TPU v7x, 512 devices: a whole 4x4x16 slice. The times are simulated.
512 devices in a mesh: gx: 32 (over x, z_hi, y), gy: 16 (over z_lo, core).
Axes of the slice: x: 4, y: 4, z: 16 (z_hi: 2, z_lo: 8; z = z_hi * 8 + z_lo), core: 2. Of those that a mesh axis runs over, the one named last changes fastest.
Arguments:
- velocity: float32 [3, 256, 256, 128], P(None, 'gx', 'gy'), may hold values from -6 to 6
- viscosity: float32 [256, 256, 128], P('gx', 'gy'), may hold values from 0.5 to 20
- pressure: float32 [256, 256, 128], P('gx', 'gy'), may hold values from -6 to 6
- flags: int32 [256, 256, 128], P('gx', 'gy'), may hold values from 0 to 2
Outputs:
- corrected: float32 [3, 256, 256, 128], P(None, 'gx', 'gy')
Inputs may be any that keep to these rules, and one draw needn't show every extreme that they name: `flags`: 0 marks solid, 1 fluid, 2 air.
All inputs are finite; a program needn't handle non-finite values.
Results may differ from a plain program's by a relative error of at most 0.00018.
Values sent between devices are 32-bit elements; how exact they have to be, the bound alone decides.
A program may use at most 64 MiB of HBM per device.

v0:
```python
import jax
import jax.numpy as jnp
from jax import lax
from jax.sharding import PartitionSpec as P

ITERS = 3


def with_halo(block, sides, width):
    for axis, dim in sides:
        count = lax.axis_size(axis)
        forward = [(i, i + 1) for i in range(count - 1)]
        backward = [(target, source) for source, target in forward]
        low = lax.ppermute(
            lax.slice_in_dim(block, block.shape[dim] - width, None, axis=dim), axis, forward
        )
        high = lax.ppermute(lax.slice_in_dim(block, 0, width, axis=dim), axis, backward)
        block = jnp.concatenate([low, block, high], axis=dim)
    return block


def shift_low(array, axis):
    widths = [(0, 0)] * array.ndim
    widths[axis] = (1, 0)
    padded = jnp.pad(array, widths)
    return jax.lax.slice_in_dim(padded, 0, array.shape[axis], axis=axis)


def coefficients(grid_fields):
    visc, press, fluid, opened = (grid_fields[0], grid_fields[1], grid_fields[2], grid_fields[3])
    cell_weight = 2.0 * visc * fluid

    def edge_weight(axis_one, axis_two):
        visc_one = shift_low(visc, axis_one)
        fluid_one = shift_low(fluid, axis_one)
        mean_visc = 0.25 * (
            visc + visc_one + shift_low(visc, axis_two) + shift_low(visc_one, axis_two)
        )
        most_fluid = jnp.maximum(
            jnp.maximum(fluid, fluid_one),
            jnp.maximum(shift_low(fluid, axis_two), shift_low(fluid_one, axis_two)),
        )
        return mean_visc * most_fluid

    weight_xy = edge_weight(0, 1)
    weight_xz = edge_weight(0, 2)
    weight_yz = edge_weight(1, 2)
    inner = (slice(1, -1), slice(1, -1), slice(1, -1))
    active = jnp.stack(
        [
            (jnp.maximum(fluid, shift_low(fluid, axis)) * opened * shift_low(opened, axis))[inner]
            for axis in range(3)
        ]
    )
    diag_u = (
        1.0
        + cell_weight[inner]
        + shift_low(cell_weight, 0)[inner]
        + weight_xy[inner]
        + weight_xy[1:-1, 2:, 1:-1]
        + weight_xz[inner]
        + weight_xz[1:-1, 1:-1, 2:]
    )
    diag_v = (
        1.0
        + cell_weight[inner]
        + shift_low(cell_weight, 1)[inner]
        + weight_xy[inner]
        + weight_xy[2:, 1:-1, 1:-1]
        + weight_yz[inner]
        + weight_yz[1:-1, 1:-1, 2:]
    )
    diag_w = (
        1.0
        + cell_weight[inner]
        + shift_low(cell_weight, 2)[inner]
        + weight_xz[inner]
        + weight_xz[2:, 1:-1, 1:-1]
        + weight_yz[inner]
        + weight_yz[1:-1, 2:, 1:-1]
    )
    diagonal = active * jnp.stack([diag_u, diag_v, diag_w]) + (1.0 - active)
    effective = press * fluid
    gradient = jnp.stack([(effective - shift_low(effective, axis))[inner] for axis in range(3)])
    return ((cell_weight, weight_xy, weight_xz, weight_yz), active, diagonal, gradient)


def energy(field, weights):
    cell_weight, weight_xy, weight_xz, weight_yz = weights
    along_u, along_v, along_w = (field[0], field[1], field[2])
    stretch_x = along_u[1:, :-1, :-1] - along_u[:-1, :-1, :-1]
    stretch_y = along_v[:-1, 1:, :-1] - along_v[:-1, :-1, :-1]
    stretch_z = along_w[:-1, :-1, 1:] - along_w[:-1, :-1, :-1]
    total = 0.5 * jnp.sum(
        cell_weight[:-1, :-1, :-1]
        * (stretch_x * stretch_x + stretch_y * stretch_y + stretch_z * stretch_z)
    )
    shear_xy = along_u[1:, 1:, :] - along_u[1:, :-1, :] + along_v[1:, 1:, :] - along_v[:-1, 1:, :]
    shear_xz = along_u[1:, :, 1:] - along_u[1:, :, :-1] + along_w[1:, :, 1:] - along_w[:-1, :, 1:]
    shear_yz = along_v[:, 1:, 1:] - along_v[:, 1:, :-1] + along_w[:, 1:, 1:] - along_w[:, :-1, 1:]
    total = total + 0.5 * jnp.sum(weight_xy[1:, 1:, :] * shear_xy * shear_xy)
    total = total + 0.5 * jnp.sum(weight_xz[1:, :, 1:] * shear_xz * shear_xz)
    total = total + 0.5 * jnp.sum(weight_yz[:, 1:, 1:] * shear_yz * shear_yz)
    return total


def preconditioned_norm(residual, scaled):
    return lax.psum(jnp.sum(residual * scaled), ("gx", "gy"))


def local(velocity, viscosity, pressure, flags):
    fluid = (flags == 1).astype(jnp.float32)
    opened = (flags != 0).astype(jnp.float32)
    stacked = jnp.stack([viscosity, pressure, fluid, opened])
    extended = with_halo(stacked, (("gx", 1), ("gy", 2)), 1)
    grid_fields = jnp.pad(extended, ((0, 0), (0, 0), (0, 0), (1, 1)))
    weights, active, diagonal, gradient = coefficients(grid_fields)

    def operate(field):
        wider = with_halo(field, (("gx", 1), ("gy", 2)), 1)
        padded = jnp.pad(wider, ((0, 0), (0, 0), (0, 0), (1, 1)))
        forces = jax.grad(energy)(padded, weights)[:, 1:-1, 1:-1, 1:-1]
        return active * (field + forces)

    started = active * (velocity - gradient)
    corrected = started
    residual = started - operate(started)
    search = residual / diagonal
    norm_now = preconditioned_norm(residual, search)
    for sweep in range(ITERS):
        image = operate(search)
        step_size = norm_now / lax.psum(jnp.sum(search * image), ("gx", "gy"))
        corrected = corrected + step_size * search
        residual = residual - step_size * image
        if sweep + 1 < ITERS:
            scaled = residual / diagonal
            norm_next = preconditioned_norm(residual, scaled)
            search = scaled + norm_next / norm_now * search
            norm_now = norm_next
    return corrected


def solution(mesh):
    in_specs = (
        P(None, "gx", "gy", None),
        P("gx", "gy", None),
        P("gx", "gy", None),
        P("gx", "gy", None),
    )
    out_specs = P(None, "gx", "gy", None)
    return jax.shard_map(local, mesh=mesh, in_specs=in_specs, out_specs=out_specs, check_vma=False)
```

profile of v0, /device:TPU:1, one launch (start us, length us, event | category | flops | bytes accessed | tf_op | source)
XLA Modules:
  0.0 688.2 jit_solution(590783157736293031)
XLA Ops:
  0.0 0.9 convert_bitcast_fusion.1
  0.9 4.0 collective-permute-start
  5.0 1.3 collective-permute-start.1
  6.3 3.3 collective-permute-done.1
  9.7 5.5 collective-permute-start.2
  15.2 3.0 collective-permute-start.3
  18.2 2.1 collective-permute-done.3
  21.8 0.4 maximum_multiply_fusion.2
  22.5 0.7 copy-done
  23.2 3.2 collective-permute-start.4
  26.4 1.3 collective-permute-start.5
  27.8 13.4 %collective-permute-done.5 = f32[3,1,16,128]{3,2,1,0:T(8,128)S(1)} collective-permute-done((f32[3,1,16,128]{3,2,1,0:T(8,128)S(1)}, f32[3,1,16,128]{3,2,1,0:T(8,128)S(1)}, u32[]{:S(2)}, u32[]{:S(2)}) %collective-permute-start.5) | collective-permute-done | bytes 24608 | tf_op jit(solution)/shard_map/ppermute | solution.py:17
  41.2 3.2 collective-permute-start.6
  44.4 1.9 collective-permute-start.7
  46.6 2.8 collective-permute-done.7
  50.8 0.5 add_bitcast_fusion.11
  51.4 14.5 %collective-permute-start.8 = (f32[3,1,16,128]{3,2,1,0:T(8,128)S(1)}, f32[3,1,16,128]{3,2,1,0:T(8,128)S(1)}, u32[]{:S(2)}, u32[]{:S(2)}) collective-permute-start(f32[3,1,16,128]{3,2,1,0:T(8,128)S(1)} %get-tuple-element.150), channel_id=1, source_target_pairs={{0,16},{16,32},{32,48},{48,64},{64,80},{80,96},{96,112},{112,128},... | collective-permute-start | bytes 73736 | tf_op jit(solution)/shard_map/ppermute | solution.py:14
  65.9 1.3 collective-permute-start.9
  67.2 3.6 collective-permute-done.9
  70.8 3.2 collective-permute-start.10
  74.0 1.9 collective-permute-start.11
  76.0 3.1 collective-permute-done.11
  80.4 0.5 add_bitcast_fusion.8
  81.0 0.7 multiply_reduce_fusion.3
  81.7 123.7 %all-reduce.95 = (f32[]{:T(128)}, f32[]{:T(128)}) all-reduce(f32[]{:T(128)} %get-tuple-element.6, f32[]{:T(128)} %get-tuple-element.5), channel_id=1, replica_groups=mesh['gx'=32,'gy'=16] {'gx','gy'}, use_global_device_ids=true, to_apply=%region_1.2 | all-reduce | flops 2 | bytes 16 | tf_op jit(solution)/shard_map/psum | solution.py:108
  206.8 0.7 multiply_reduce_fusion.2
  207.4 98.9 %psum.44 = f32[]{:T(128)} all-reduce(f32[]{:T(128)} %get-tuple-element.35), channel_id=1, replica_groups=mesh['gx'=32,'gy'=16] {'gx','gy'}, use_global_device_ids=true, to_apply=%region_5.6 | all-reduce | flops 1 | bytes 8 | tf_op jit(solution)/shard_map/psum | solution.py:108
  307.7 2.8 collective-permute-start.12
  310.5 1.3 collective-permute-start.13
  311.8 3.3 collective-permute-done.13
  315.1 5.6 collective-permute-start.14
  320.7 1.9 collective-permute-start.15
  322.6 3.1 collective-permute-done.15
  327.1 0.5 add_bitcast_fusion.5
  327.7 0.7 multiply_reduce_fusion.1
  328.4 117.7 %psum.45 = f32[]{:T(128)} all-reduce(f32[]{:T(128)} %get-tuple-element.21), channel_id=1, replica_groups=mesh['gx'=32,'gy'=16] {'gx','gy'}, use_global_device_ids=true, to_apply=%region_7.8 | all-reduce | flops 1 | bytes 8 | tf_op jit(solution)/shard_map/psum | solution.py:132
  447.5 0.7 multiply_reduce_fusion
  448.1 99.6 %psum.46 = f32[]{:T(128)} all-reduce(f32[]{:T(128)} %multiply_reduce_fusion), channel_id=1, replica_groups=mesh['gx'=32,'gy'=16] {'gx','gy'}, use_global_device_ids=true, to_apply=%region_9.10 | all-reduce | flops 1 | bytes 8 | tf_op jit(solution)/shard_map/psum | solution.py:108
  549.1 2.7 collective-permute-start.16
  551.8 1.3 collective-permute-start.17
  553.1 3.3 collective-permute-done.17
  556.4 5.6 collective-permute-start.18
  562.0 1.9 collective-permute-start.19
  563.9 3.1 collective-permute-done.19
  568.4 0.5 add_bitcast_fusion.2
  568.9 0.7 fusion.33
  569.7 116.5 %psum.47 = f32[]{:T(128)} all-reduce(f32[]{:T(128)} %fusion.33), channel_id=1, replica_groups=mesh['gx'=32,'gy'=16] {'gx','gy'}, use_global_device_ids=true, to_apply=%region_11.12 | all-reduce | flops 1 | bytes 8 | tf_op jit(solution)/shard_map/psum | solution.py:132
  687.4 0.8 multiply_add_fusion.12
  (63 shorter events, 7.7 us)
Async XLA Ops:
  0.0 0.9 copy-start.1
  0.0 0.9 copy-start.2
  0.9 5.3 collective-permute-start
  5.0 4.7 collective-permute-start.1
  9.7 8.5 %collective-permute-start.2 = (f32[4,10,1,128]{3,2,1,0:T(1,128)S(1)}, f32[4,10,1,128]{3,2,1,0:T(1,128)S(1)}, u32[]{:S(2)}, u32[]{:S(2)}) collective-permute-start(f32[4,10,1,128]{3,2,1,0:T(1,128)S(1)} %get-tuple-element.103), channel_id=1, source_target_pairs={{0,1},{1,2},{2,3},{3,4},{4,5},{5,6},{6,7},{7,8},{8,9},{9,10},{10,1... | collective-permute-start | bytes 61448 | tf_op jit(solution)/shard_map/ppermute | solution.py:14
  15.2 5.1 collective-permute-start.3
  22.2 0.9 copy-start
  23.2 4.5 collective-permute-start.4
  26.4 14.7 %collective-permute-start.5 = (f32[3,1,16,128]{3,2,1,0:T(8,128)S(1)}, f32[3,1,16,128]{3,2,1,0:T(8,128)S(1)}, u32[]{:S(2)}, u32[]{:S(2)}) collective-permute-start(f32[3,1,16,128]{3,2,1,0:T(8,128)S(1)} %get-tuple-element.153), channel_id=1, source_target_pairs={{16,0},{32,16},{48,32},{64,48},{80,64},{96,80},{112,96},{128,112},... | collective-permute-start | bytes 73736 | tf_op jit(solution)/shard_map/ppermute | solution.py:17
  41.2 5.4 collective-permute-start.6
  44.4 5.0 collective-permute-start.7
  51.4 15.8 %collective-permute-start.8 = (f32[3,1,16,128]{3,2,1,0:T(8,128)S(1)}, f32[3,1,16,128]{3,2,1,0:T(8,128)S(1)}, u32[]{:S(2)}, u32[]{:S(2)}) collective-permute-start(f32[3,1,16,128]{3,2,1,0:T(8,128)S(1)} %get-tuple-element.150), channel_id=1, source_target_pairs={{0,16},{16,32},{32,48},{48,64},{64,80},{80,96},{96,112},{112,128},... | collective-permute-start | bytes 73736 | tf_op jit(solution)/shard_map/ppermute | solution.py:14
  65.9 4.9 collective-permute-start.9
  70.8 5.2 collective-permute-start.10
  74.0 5.0 collective-permute-start.11
  307.7 4.1 collective-permute-start.12
  310.5 4.6 collective-permute-start.13
  315.1 7.6 %collective-permute-start.14 = (f32[3,10,1,128]{3,2,1,0:T(1,128)S(1)}, f32[3,10,1,128]{3,2,1,0:T(1,128)S(1)}, u32[]{:S(2)}, u32[]{:S(2)}) collective-permute-start(f32[3,10,1,128]{3,2,1,0:T(1,128)S(1)} %get-tuple-element.117), channel_id=1, source_target_pairs={{0,1},{1,2},{2,3},{3,4},{4,5},{5,6},{6,7},{7,8},{8,9},{9,10},{10,1... | collective-permute-start | bytes 46088 | tf_op jit(solution)/shard_map/ppermute | solution.py:14
  320.7 5.0 collective-permute-start.15
  549.1 4.0 collective-permute-start.16
  551.8 4.6 collective-permute-start.17
  556.4 7.5 %collective-permute-start.18 = (f32[3,10,1,128]{3,2,1,0:T(1,128)S(1)}, f32[3,10,1,128]{3,2,1,0:T(1,128)S(1)}, u32[]{:S(2)}, u32[]{:S(2)}) collective-permute-start(f32[3,10,1,128]{3,2,1,0:T(1,128)S(1)} %get-tuple-element.111), channel_id=1, source_target_pairs={{0,1},{1,2},{2,3},{3,4},{4,5},{5,6},{6,7},{7,8},{8,9},{9,10},{10,1... | collective-permute-start | bytes 46088 | tf_op jit(solution)/shard_map/ppermute | solution.py:14
  562.0 5.0 collective-permute-start.19
where the time goes:
time: 690 us; the launch traced here: 688 us
  blocking collectives  556 us (81%)
  starting transfers between devices  67.4 us (10%)
  waiting for transfers between devices  41.1 us (6%)
  other arithmetic  14.6 us (2%)
  between operations  7.17 us (1%)
    psum x3, blocking collectives, preconditioned_norm(): return lax.psum(jnp.sum(residual * scaled), ('gx', 'gy'))  322 us
    psum x2, blocking collectives, local(): step_size = norm_now / lax.psum(jnp.sum(search * image), ('gx', 'gy'))  234 us
    ppermute x10, starting transfers between devices, with_halo(): lax.ppermute(lax.slice_in_dim(block, block.shape[dim] - width, None, axis...  50.3 us
    ppermute x10, waiting for transfers between devices, with_halo(): lax.ppermute(lax.slice_in_dim(block, 0, width, axis=dim), axis, backward)  41.1 us
    ppermute x10, starting transfers between devices, with_halo(): lax.ppermute(lax.slice_in_dim(block, 0, width, axis=dim), axis, backward)  17.1 us
  transfers between devices with their start and end apart: 20, of which 10 were waited for; matrix products, arithmetic and copies ran while one was open for 0% of the time, Pallas kernels for 0%

commit v1 on v0

v1 whole, which is shorter than its diff:
```python
import jax
import jax.numpy as jnp
from jax import lax
from jax.experimental import pallas as pl
from jax.experimental.pallas import tpu as pltpu
from jax.sharding import PartitionSpec as P

MESH = pl.DeviceIdType.MESH
F32 = jnp.float32
NX, NY, NZ = 8, 16, 128
LOW, HIGH = 4, 3
EX, EY = NX + LOW + HIGH, 24
X0, X1 = LOW, LOW + NX
Y0, Y1 = LOW, LOW + NY
CARD, RING = 32, 16


def low_y(a):
    return pltpu.roll(a, 1, 1)


def next_y(a):
    return pltpu.roll(a, EY - 1, 1)


def lanes(a):
    return lax.broadcasted_iota(jnp.int32, a.shape, a.ndim - 1)


def low_z(a):
    return jnp.where(lanes(a) == 0, 0.0, pltpu.roll(a, 1, a.ndim - 1))


def next_z(a):
    return jnp.where(lanes(a) == NZ - 1, 0.0, pltpu.roll(a, NZ - 1, a.ndim - 1))


def blocks(start, stop, size):
    count = -(-(stop - start) // size)
    edges = [start + (stop - start) * n // count for n in range(count + 1)]
    return list(zip(edges[:-1], edges[1:]))


def kernel(
    gxn, gyn,
    vel, visc, press, flags, out,
    S, V0, V1, V2, VEL, VI, FL, PR, RAW, RAWIN,
    CW, WXY, WXZ, WYZ, EU, EV, DU, DV, DW,
    CARDS, RINGS,
    lsem, xs, xr, ys, yr, cs, cr, rs, rr,
):
    gx, gy = lax.axis_index("gx"), lax.axis_index("gy")
    has_xlo, has_xhi = gx > 0, gx < gxn - 1
    has_ylo, has_yhi = gy > 0, gy < gyn - 1
    xlo, xhi = (gx - 1, gy), (gx + 1, gy)
    ylo, yhi = (gx, gy - 1), (gx, gy + 1)
    px, zh, py = gx // 8, lax.rem(gx // 4, 2), lax.rem(gx, 4)
    zl, core = gy // 2, lax.rem(gy, 2)
    card = (px * 4 + py) * 2 + core
    ring = zh * 8 + zl

    def card_device(r):
        return ((r // 8) * 8 + zh * 4 + lax.rem(r // 2, 4), zl * 2 + lax.rem(r, 2))

    def ring_device(r):
        return (px * 8 + (r // 8) * 4 + py, lax.rem(r, 8) * 2 + core)

    own = (pl.ds(X0, NX), pl.ds(Y0, NY))
    local = [
        pltpu.make_async_copy(flags, FL.at[own], lsem.at[0]),
        pltpu.make_async_copy(press, PR.at[pl.ds(1, NX), pl.ds(Y0, NY)], lsem.at[1]),
        pltpu.make_async_copy(vel, VEL.at[:, :, pl.ds(Y0, NY)], lsem.at[2]),
        pltpu.make_async_copy(visc, VI.at[own], lsem.at[3]),
    ]
    for copy in local:
        copy.start()

    def clear(ref, lead, kind):
        zero = lambda *shape: jnp.zeros(shape, kind)
        for c in range(lead) if lead else [None]:
            at = ref if c is None else ref.at[c]
            at[0:X0] = zero(X0, EY, NZ)
            at[X1:EX] = zero(EX - X1, EY, NZ)
            at[X0:X1, 0:Y0] = zero(NX, Y0, NZ)
            at[X0:X1, Y1:EY] = zero(NX, EY - Y1, NZ)

    clear(S, 3, F32)
    clear(VI, 0, F32)
    clear(FL, 0, jnp.int32)
    PR[0] = jnp.zeros((EY, NZ), F32)
    PR[1:, 0:Y0] = jnp.zeros((NX, Y0, NZ), F32)
    PR[1:, Y1:EY] = jnp.zeros((NX, EY - Y1, NZ), F32)
    RAWIN[...] = jnp.zeros((1, EY, NZ), F32)
    for c in range(3):
        V2[c, X1] = jnp.zeros((EY, NZ), F32)
        VEL[c, :, 0:Y0] = jnp.zeros((NX, Y0, NZ), F32)
        VEL[c, :, Y1:EY] = jnp.zeros((NX, EY - Y1, NZ), F32)

    barrier = pltpu.get_barrier_semaphore()

    def greet(device):
        pl.semaphore_signal(barrier, inc=1, device_id=device, device_id_type=MESH)

    near = [(has_xlo, xlo), (has_xhi, xhi), (has_ylo, ylo), (has_yhi, yhi)]
    for there, device in near:
        pl.when(there)(lambda device=device: greet(device))

    @pl.loop(1, CARD)
    def _(d):
        greet(card_device(lax.rem(card + d, CARD)))

    @pl.loop(1, RING)
    def _(d):
        greet(ring_device(lax.rem(ring + d, RING)))

    one = lambda there: jnp.where(there, 1, 0)
    pl.semaphore_wait(barrier, CARD + RING - 2 + sum(one(t) for t, _ in near))

    sent = []

    def send(source, target, sems, n, to, there, from_):
        copy = pltpu.make_async_remote_copy(
            src_ref=source, dst_ref=target, send_sem=sems[0].at[n], recv_sem=sems[1].at[n],
            device_id=to, device_id_type=MESH,
        )
        pl.when(there)(copy.start)
        sent.append((there, copy))
        return lambda: pl.when(from_)(copy.wait_recv)

    X, Y = (xs, xr), (ys, yr)
    UP, DOWN = (xhi, has_xhi, has_xlo), (xlo, has_xlo, has_xhi)
    NORTH, SOUTH = (yhi, has_yhi, has_ylo), (ylo, has_ylo, has_yhi)
    rows = pl.ds(Y0, NY)
    last4, first3 = pl.ds(NX - LOW, LOW), pl.ds(0, HIGH)
    xlow, xhigh, xown = pl.ds(0, LOW), pl.ds(X1, HIGH), pl.ds(X0, NX)
    ylow, yhigh = pl.ds(0, LOW), pl.ds(Y1, HIGH)
    ylast, yfirst = pl.ds(NY - LOW, LOW), pl.ds(0, HIGH)
    elast, efirst = pl.ds(Y1 - LOW, LOW), pl.ds(Y0, HIGH)

    x_cells = [
        send(flags.at[last4], FL.at[xlow, rows], X, 0, *UP),
        send(flags.at[first3], FL.at[xhigh, rows], X, 1, *DOWN),
        send(visc.at[last4], VI.at[xlow, rows], X, 2, *UP),
        send(visc.at[first3], VI.at[xhigh, rows], X, 3, *DOWN),
    ]
    x_press = send(press.at[pl.ds(NX - 1, 1)], PR.at[pl.ds(0, 1), rows], X, 4, *UP)
    y_press = send(press.at[:, pl.ds(NY - 1, 1)], PR.at[pl.ds(1, NX), pl.ds(Y0 - 1, 1)], Y, 0, *NORTH)
    y_flags = send(flags.at[:, ylast], FL.at[xown, ylow], Y, 1, *NORTH)
    y_cells = [
        send(flags.at[:, yfirst], FL.at[xown, yhigh], Y, 2, *SOUTH),
        send(visc.at[:, ylast], VI.at[xown, ylow], Y, 3, *NORTH),
        send(visc.at[:, yfirst], VI.at[xown, yhigh], Y, 4, *SOUTH),
    ]

    for copy in local[:3]:
        copy.wait()
    y_press()
    y_flags()
    y_cells.pop(0)()

    def is_fluid(f):
        return jnp.where(f == 1, 1.0, 0.0)

    def is_open(f):
        return jnp.where(f != 0, 1.0, 0.0)

    for a, b in blocks(X0, X1, 4):
        f = FL[a:b]
        fluid, opened = is_fluid(f), is_open(f)
        p = PR[a - LOW + 1 : b - LOW + 1] * fluid
        act = jnp.maximum(fluid, low_y(fluid)) * opened * low_y(opened)
        S[1, a:b, Y0:Y1] = (act * (VEL[1, a - X0 : b - X0] - (p - low_y(p))))[:, Y0:Y1]
        act = jnp.maximum(fluid, low_z(fluid)) * opened * low_z(opened)
        S[2, a:b, Y0:Y1] = (act * (VEL[2, a - X0 : b - X0] - (p - low_z(p))))[:, Y0:Y1]
        if a == X0:
            RAW[...] = VEL[0, 0:1] - p[0:1]
            fluid, opened, p, a = fluid[1:], opened[1:], p[1:], a + 1
        below = FL[a - 1 : b - 1]
        fluid_below = is_fluid(below)
        p_below = PR[a - LOW : b - LOW] * fluid_below
        act = jnp.maximum(fluid, fluid_below) * opened * is_open(below)
        S[0, a:b, Y0:Y1] = (act * (VEL[0, a - X0 : b - X0] - (p - p_below)))[:, Y0:Y1]

    vw = pl.ds(1, 2)
    x_started = [
        send(S.at[:, pl.ds(X1 - LOW, LOW), rows], S.at[:, xlow, rows], X, 5, *UP),
        send(S.at[vw, pl.ds(X0, HIGH), rows], S.at[vw, xhigh, rows], X, 6, *DOWN),
        send(S.at[0, pl.ds(X0 + 1, HIGH - 1), rows], S.at[0, pl.ds(X1 + 1, HIGH - 1), rows], X, 7, *DOWN),
        send(RAW.at[:, rows], RAWIN.at[:, rows], X, 8, *DOWN),
    ]
    upper = pl.ds(X0 + 1, NX - 1)
    y_started = [
        send(S.at[vw, xown, elast], S.at[vw, xown, ylow], Y, 5, *NORTH),
        send(S.at[0, upper, elast], S.at[0, upper, ylow], Y, 6, *NORTH),
        send(S.at[vw, xown, efirst], S.at[vw, xown, yhigh], Y, 7, *SOUTH),
        send(S.at[0, upper, efirst], S.at[0, upper, yhigh], Y, 8, *SOUTH),
    ]

    local[3].wait()
    n = 9
    for wait in x_cells:
        wait()
    for ref in (FL, VI):
        for layers in (xlow, xhigh):
            y_cells.append(send(ref.at[layers, elast], ref.at[layers, ylow], Y, n, *NORTH))
            y_cells.append(send(ref.at[layers, efirst], ref.at[layers, yhigh], Y, n + 1, *SOUTH))
            n += 2
    for wait in y_cells:
        wait()

    for a, b in blocks(1, EX, 5):
        f = is_fluid(FL[a - 1 : b])
        m = VI[a - 1 : b]
        fx, mx = jnp.maximum(f[1:], f[:-1]), m[1:] + m[:-1]
        fc, mc = f[1:], m[1:]
        if a == 1:
            CW[0] = 2.0 * m[0] * f[0]
        CW[a:b] = 2.0 * mc * fc
        WXY[a:b] = 0.25 * (mx + low_y(mx)) * jnp.maximum(fx, low_y(fx))
        WXZ[a:b] = 0.25 * (mx + low_z(mx)) * jnp.maximum(fx, low_z(fx))
        fy, my = jnp.maximum(fc, low_y(fc)), mc + low_y(mc)
        WYZ[a:b] = 0.25 * (my + low_z(my)) * jnp.maximum(fy, low_z(fy))
        top = lanes(fx) == NZ - 1
        EU[a:b] = jnp.where(top, 0.25 * mx * fx, 0.0)
        EV[a:b] = jnp.where(top, 0.25 * my * fy, 0.0)
    for a, b in blocks(1, EX - 1, 5):
        f = FL[a - 1 : b]
        fluid, opened = is_fluid(f), is_open(f)
        fc, oc = fluid[1:], opened[1:]
        cw = CW[a:b]
        wxy, wxz, wyz = WXY[a : b + 1], WXZ[a : b + 1], WYZ[a:b]
        xy, xz = wxy[:-1], wxz[:-1]
        act = jnp.maximum(fc, fluid[:-1]) * oc * opened[:-1]
        DU[a:b] = act / (1.0 + cw + CW[a - 1 : b - 1] + xy + next_y(xy) + xz + next_z(xz) + EU[a:b])
        act = jnp.maximum(fc, low_y(fc)) * oc * low_y(oc)
        DV[a:b] = act / (1.0 + cw + low_y(cw) + xy + wxy[1:] + wyz + next_z(wyz) + EV[a:b])
        act = jnp.maximum(fc, low_z(fc)) * oc * low_z(oc)
        DW[a:b] = act / (1.0 + cw + low_z(cw) + xz + wxz[1:] + wyz + next_y(wyz))

    for wait in x_started:
        wait()
    x_press()
    for layer, below, raw in ((X0, PR[0:1], RAW[...]), (X1, PR[NX : NX + 1], RAWIN[...])):
        f, g = FL[layer : layer + 1], FL[layer - 1 : layer]
        act = jnp.maximum(is_fluid(f), is_fluid(g)) * is_open(f) * is_open(g)
        S[0, layer : layer + 1, Y0:Y1] = (act * (raw + below * is_fluid(g)))[:, Y0:Y1]
    lowest = pl.ds(X0, 1)
    for there, at in ((S, (slice(None), xlow)), (S, (slice(None), xhigh)), (S, (0, lowest))):
        y_started.append(send(there.at[(*at, elast)], there.at[(*at, ylow)], Y, n, *NORTH))
        y_started.append(send(there.at[(*at, efirst)], there.at[(*at, yhigh)], Y, n + 1, *SOUTH))
        n += 2
    for wait in y_started:
        wait()

    def gradient(F, a, b):
        u, v, w = F[0, a - 1 : b + 1], F[1, a - 1 : b + 1], F[2, a - 1 : b + 1]
        uc, vc, wc = u[1:-1], v[1:-1], w[1:-1]
        sx = CW[a - 1 : b] * (u[1:] - u[:-1])
        un, vn, wn = u[1:], v[1:], w[1:]
        xy = WXY[a : b + 1] * (un - low_y(un) + vn - v[:-1])
        xz = WXZ[a : b + 1] * (un - low_z(un) + wn - w[:-1])
        cw = CW[a:b]
        sy = cw * (next_y(vc) - vc)
        sz = cw * (next_z(wc) - wc)
        yz = WYZ[a:b] * (vc - low_z(vc) + wc - low_y(wc))
        xyc, xzc = xy[:-1], xz[:-1]
        return (
            sx[:-1] - sx[1:] + xyc - next_y(xyc) + xzc - next_z(xzc) + EU[a:b] * uc,
            low_y(sy) - sy + xyc - xy[1:] + yz - next_z(yz) + EV[a:b] * vc,
            low_z(sz) - sz + xzc - xz[1:] + yz - next_y(yz),
        ), (uc, vc, wc)

    D = (DU, DV, DW)
    row = lax.broadcasted_iota(jnp.int32, (1, EY, NZ), 1)
    inside = (row >= Y0) & (row < Y1)

    def partial(values, a, b, mask):
        lo, hi = max(a, X0), min(b, X1)
        if lo >= hi:
            return jnp.zeros((1, EY, NZ), F32)
        part = values[lo - a : hi - a]
        return jnp.where(mask, jnp.sum(part, axis=0, keepdims=True), 0.0)

    zero = jnp.zeros((1, EY, NZ), F32)
    b0 = h00 = h01 = h11 = h12 = h22 = zero
    for a, b in blocks(1, EX - 1, 4):
        grad, _ = gradient(S, a, b)
        total = 0.0
        for c in range(3):
            z = -D[c][a:b] * grad[c]
            V0[c, a:b] = z
            total = total - z * grad[c]
        b0 = b0 + partial(total, a, b, inside)
    for a, b in blocks(2, EX - 2, 4):
        grad, field = gradient(V0, a, b)
        same = cross = 0.0
        for c in range(3):
            g = field[c] + grad[c]
            z = D[c][a:b] * g - field[c]
            V1[c, a:b] = z
            same, cross = same + field[c] * g, cross + z * g
        h00, h01 = h00 + partial(same, a, b, inside), h01 + partial(cross, a, b, inside)
    for a, b in blocks(3, EX - 3, 4):
        grad, field = gradient(V1, a, b)
        same = cross = 0.0
        for c in range(3):
            g = field[c] + grad[c]
            z = D[c][a:b] * g - field[c]
            V2[c, a:b] = z
            same, cross = same + field[c] * g, cross + z * g
        h11, h12 = h11 + partial(same, a, b, inside), h12 + partial(cross, a, b, inside)
    edge = row == Y1
    upto = inside | (edge & jnp.logical_not(has_yhi))
    below = ((row >= Y0 - 1) & (row < Y1 - 1)) | ((row == Y1 - 1) & jnp.logical_not(has_yhi))
    for a, b in blocks(X0, X1 + 1, 5):
        u, v, w = V2[0, a - 1 : b], V2[1, a - 1 : b], V2[2, a - 1 : b]
        uc, vc, wc = u[1:], v[1:], w[1:]
        cw = CW[a - 1 : b]
        dx = uc - u[:-1]
        xy = uc - low_y(uc) + vc - v[:-1]
        xz = uc - low_z(uc) + wc - w[:-1]
        yz = vc - low_z(vc) + wc - low_y(wc)
        dz = next_z(wc) - wc
        dy = next_y(vc) - vc
        most = (
            cw[:-1] * dx * dx + WXY[a:b] * xy * xy + WXZ[a:b] * xz * xz + WYZ[a:b] * yz * yz
            + cw[1:] * dz * dz + (1.0 + EU[a:b]) * uc * uc + (1.0 + EV[a:b]) * vc * vc + wc * wc
        )
        along = cw[1:] * dy * dy
        value = jnp.where(upto, most, 0.0) + jnp.where(below, along, 0.0)
        h22 = h22 + jnp.sum(value[: min(b, X1) - a], axis=0, keepdims=True)
        if b > X1:
            h22 = h22 + jnp.where(has_xhi, 0.0, value[X1 - a : X1 - a + 1])

    lane = lax.broadcasted_iota(jnp.int32, (1, NZ), 1)
    payload = jnp.zeros((1, NZ), F32)
    for k, value in enumerate((b0, h00, h01, h11, h12, h22)):
        total = jnp.sum(jnp.sum(value[0], axis=0, keepdims=True), axis=1, keepdims=True)
        payload = jnp.where(lane == k, total, payload)

    def gather(slots, count, me, device, sends, recvs, value):
        slots[me] = value
        copy = lambda peer: pltpu.make_async_remote_copy(
            src_ref=slots.at[me], dst_ref=slots.at[me], send_sem=sends.at[peer], recv_sem=recvs.at[me],
            device_id=device(peer), device_id_type=MESH,
        )
        arrival = lambda peer: pltpu.make_async_remote_copy(
            src_ref=slots.at[me], dst_ref=slots.at[peer], send_sem=sends.at[peer], recv_sem=recvs.at[peer],
            device_id=device(peer), device_id_type=MESH,
        )

        @pl.loop(1, count)
        def _(d):
            copy(lax.rem(me + d, count)).start()

        @pl.loop(1, count)
        def _(d):
            arrival(lax.rem(me + d, count)).wait_recv()

        def finish():
            @pl.loop(1, count)
            def _(d):
                copy(lax.rem(me + d, count)).wait_send()

        total = slots[0]
        for r in range(1, count):
            total = total + slots[r]
        return total, finish

    total, finish_cards = gather(CARDS, CARD, card, card_device, cs, cr, payload)
    total, finish_rings = gather(RINGS, RING, ring, ring_device, rs, rr, total)

    wide = jnp.broadcast_to(total, (8, NZ))
    at = lax.broadcasted_iota(jnp.int32, (8, NZ), 1)
    m = [
        jnp.broadcast_to(jnp.sum(jnp.where(at == k, wide, 0.0), axis=1, keepdims=True), (8, NZ))
        for k in range(6)
    ]
    r0, a00, a01, a11, a12, a22 = m
    r1 = a00 - r0
    r2 = a01 - r1
    a02 = a11
    tiny = 1e-6

    def over(top, pivot, size):
        good = pivot > tiny * size
        return jnp.where(good, top / jnp.where(good, pivot, 1.0), 0.0)

    d0 = a00
    l10, l20 = over(a01, d0, 0.0), over(a02, d0, 0.0)
    d1 = a11 - l10 * a01
    e21 = a12 - l20 * a01
    l21 = over(e21, d1, a11)
    d2 = a22 - l20 * a02 - l21 * e21
    y1 = r1 - l10 * r0
    y2 = r2 - l20 * r0 - l21 * y1
    c2 = over(y2, d2, a22)
    c1 = over(y1, d1, a11) - l21 * c2
    c0 = over(r0, d0, 0.0) - l10 * c1 - l20 * c2
    c0, c1, c2 = c0[0:1], c1[0:1], c2[0:1]
    for c in range(3):
        for a, b in blocks(X0, X1, 4):
            out[c, a - X0 : b - X0] = (
                S[c, a:b, Y0:Y1] + c0 * V0[c, a:b, Y0:Y1] + c1 * V1[c, a:b, Y0:Y1] + c2 * V2[c, a:b, Y0:Y1]
            )
    for there, copy in sent:
        pl.when(there)(copy.wait_send)
    finish_cards()
    finish_rings()


def solution(mesh):
    gxn, gyn = mesh.shape["gx"], mesh.shape["gy"]
    block, cells = P(None, "gx", "gy", None), P("gx", "gy", None)
    ext = (EX, EY, NZ)
    field = lambda *shape: pltpu.VMEM(shape, F32)
    dma = lambda n: pltpu.SemaphoreType.DMA((n,))

    def local(velocity, viscosity, pressure, flags):
        def body(*refs):
            kernel(gxn, gyn, *refs)

        return pl.pallas_call(
            body,
            out_shape=jax.ShapeDtypeStruct((3, NX, NY, NZ), F32),
            in_specs=[pl.BlockSpec(memory_space=pl.ANY)] * 4,
            out_specs=pl.BlockSpec(memory_space=pltpu.VMEM),
            scratch_shapes=[
                *[field(3, *ext)] * 4, field(3, NX, EY, NZ), field(*ext), pltpu.VMEM(ext, jnp.int32),
                field(NX + 1, EY, NZ), field(1, EY, NZ), field(1, EY, NZ),
                *[field(*ext)] * 9,
                field(CARD, 1, NZ), field(RING, 1, NZ),
                dma(4), dma(9), dma(9), dma(23), dma(23), dma(CARD), dma(CARD), dma(RING), dma(RING),
            ],
            compiler_params=pltpu.CompilerParams(
                collective_id=1, has_side_effects=True, vmem_limit_bytes=48 * 2**20
            ),
        )(velocity, viscosity, pressure, flags)

    return jax.shard_map(local, mesh=mesh, in_specs=(block, cells, cells, cells), out_specs=block, check_vma=False)
```

time: 690 us -> 62.3 us (0.09)
  blocking collectives: 556 us -> 0 us
  starting transfers between devices: 67.4 us -> 0 us
  Pallas kernels: 0 us -> 57.9 us
  waiting for transfers between devices: 41.1 us -> 0 us
  other arithmetic: 14.6 us -> 0 us
  between operations: 7.17 us -> 0.01 us
    psum x5 -> x0, blocking collectives: 556 us -> none  [the longest x3 322 us: preconditioned_norm(): return lax.psum(jnp.sum(residual * scaled), ('gx', 'gy'))]
    ppermute x20 -> x0, starting transfers between devices: 67.4 us -> none  [the longest x10 50.3 us: with_halo(): lax.ppermute(lax.slice_in_dim(block, block.shape[dim] - width, None, axis...]
    pallas_call x0 -> x1, Pallas kernels: none -> 57.9 us  [local(): pl.pallas_call(body, out_shape=jax.ShapeDtypeStruct((3, NX, NY, NZ), F32)...]
    ppermute x20 -> x0, waiting for transfers between devices: 41.1 us -> none  [the longest x10 41.1 us: with_halo(): lax.ppermute(lax.slice_in_dim(block, 0, width, axis=dim), axis, backward)]
  transfers between devices with their start and end apart: 20 -> 0, of which waited for: 10 -> 0; matrix products, arithmetic and copies ran while one was open for 0% -> 0% of each run, Pallas kernels for 0% -> 0%
where the time goes in v1:
time: 62.3 us; the launch traced here: 62 us
  Pallas kernels  57.9 us (93%)
  local copies, waits for them, and re-layouts  4.12 us (7%)
    pallas_call x1, Pallas kernels, local(): pl.pallas_call(body, out_shape=jax.ShapeDtypeStruct((3, NX, NY, NZ), F32)...  57.9 us
    unnamed x9, local copies, waits for them, and re-layouts  4.12 us

profile of v1, /device:TPU:1, one launch (start us, length us, event | category | flops | bytes accessed | tf_op | source)
XLA Modules:
  0.0 62.0 jit_solution(4588211975433129352)
XLA Ops:
  0.0 0.0 copy-start
  0.0 0.9 %copy-done = f32[3,8,16,128]{3,2,1,0:T(8,128)S(1)} copy-done((f32[3,8,16,128]{3,2,1,0:T(8,128)S(1)}, f32[3,8,16,128]{3,2,1,0:T(8,128)}, u32[]{:S(2)}) %copy-start) | copy-done | bytes 196632
  0.9 0.0 copy-start.1
  0.9 0.8 %copy-done.1 = f32[8,16,128]{2,1,0:T(8,128)S(1)} copy-done((f32[8,16,128]{2,1,0:T(8,128)S(1)}, f32[8,16,128]{2,1,0:T(8,128)}, u32[]{:S(2)}) %copy-start.1) | copy-done | bytes 65560
  1.8 0.0 copy-start.2
  1.8 0.8 %copy-done.2 = f32[8,16,128]{2,1,0:T(8,128)S(1)} copy-done((f32[8,16,128]{2,1,0:T(8,128)S(1)}, f32[8,16,128]{2,1,0:T(8,128)}, u32[]{:S(2)}) %copy-start.2) | copy-done | bytes 65560
  2.6 0.0 copy-start.3
  2.6 0.8 %copy-done.3 = s32[8,16,128]{2,1,0:T(8,128)S(1)} copy-done((s32[8,16,128]{2,1,0:T(8,128)S(1)}, s32[8,16,128]{2,1,0:T(8,128)}, u32[]{:S(2)}) %copy-start.3) | copy-done | bytes 65560
  3.4 57.9 %shard_map.46 = f32[3,8,16,128]{3,2,1,0:T(8,128)S(1)} custom-call(f32[3,8,16,128]{3,2,1,0:T(8,128)S(1)} %copy-done, f32[8,16,128]{2,1,0:T(8,128)S(1)} %copy-done.1, f32[8,16,128]{2,1,0:T(8,128)S(1)} %copy-done.2, s32[8,16,128]{2,1,0:T(8,128)S(1)} %copy-done.3), custom_call_target="tpu_custom_call" | custom-call | tf_op jit(solution)/shard_map/pallas_call | solution.py:423
  61.3 0.7 %copy.6 = f32[3,8,16,128]{3,2,1,0:T(8,128)} copy(f32[3,8,16,128]{3,2,1,0:T(8,128)S(1)} %shard_map.46) | data formatting | bytes 393216
Async XLA Ops:
  0.0 0.9 %copy-start = (f32[3,8,16,128]{3,2,1,0:T(8,128)S(1)}, f32[3,8,16,128]{3,2,1,0:T(8,128)}, u32[]{:S(2)}) copy-start(f32[3,8,16,128]{3,2,1,0:T(8,128)} %refs_0_.1) | copy-start | bytes 589828
  0.9 0.8 %copy-start.1 = (f32[8,16,128]{2,1,0:T(8,128)S(1)}, f32[8,16,128]{2,1,0:T(8,128)}, u32[]{:S(2)}) copy-start(f32[8,16,128]{2,1,0:T(8,128)} %refs_1_.1) | copy-start | bytes 196612
  1.8 0.8 %copy-start.2 = (f32[8,16,128]{2,1,0:T(8,128)S(1)}, f32[8,16,128]{2,1,0:T(8,128)}, u32[]{:S(2)}) copy-start(f32[8,16,128]{2,1,0:T(8,128)} %refs_2_.1) | copy-start | bytes 196612
  2.6 0.8 %copy-start.3 = (s32[8,16,128]{2,1,0:T(8,128)S(1)}, s32[8,16,128]{2,1,0:T(8,128)}, u32[]{:S(2)}) copy-start(s32[8,16,128]{2,1,0:T(8,128)} %refs_3_.1) | copy-start | bytes 196612

commit v2 on v1

--- a/solution.py
+++ b/solution.py
@@ -44,10 +44,10 @@
 def kernel(
     gxn, gyn,
     vel, visc, press, flags, out,
-    S, V0, V1, V2, VEL, VI, FL, PR, RAW, RAWIN,
+    S, V0, V1, V2, VEL, VI, FL, PR, RAW, RAWIN, VIA, FLA,
     CW, WXY, WXZ, WYZ, EU, EV, DU, DV, DW,
     CARDS, RINGS,
-    lsem, xs, xr, ys, yr, cs, cr, rs, rr,
+    lsem, xs, xr, ys, yr, gs, gr,
 ):
     gx, gy = lax.axis_index("gx"), lax.axis_index("gy")
     has_xlo, has_xhi = gx > 0, gx < gxn - 1
@@ -59,17 +59,23 @@
     card = (px * 4 + py) * 2 + core
     ring = zh * 8 + zl
 
-    def card_device(r):
-        return ((r // 8) * 8 + zh * 4 + lax.rem(r // 2, 4), zl * 2 + lax.rem(r, 2))
-
-    def ring_device(r):
-        return (px * 8 + (r // 8) * 4 + py, lax.rem(r, 8) * 2 + core)
+    def hops(d, n):
+        return min(d, n - d)
+
+    steps = [(dx, dy, dc) for dx in range(4) for dy in range(4) for dc in range(2)]
+    steps.sort(key=lambda d: -(hops(d[0], 4) + hops(d[1], 4) + 0.3 * d[2]))
+    pxs, pys, cores = [lax.rem(px + d, 4) * 8 for d in range(4)], [lax.rem(py + d, 4) for d in range(4)], (core, 1 - core)
+    card_peers = [(pxs[dx] + zh * 4 + pys[dy], zl * 2 + cores[dc]) for dx, dy, dc in steps[:-1]]
+    ring_peers = []
+    for d in sorted(range(1, RING), key=lambda d: -hops(d, RING)):
+        z = lax.rem(ring + d, RING)
+        ring_peers.append((px * 8 + (z // 8) * 4 + py, lax.rem(z, 8) * 2 + core))
 
     own = (pl.ds(X0, NX), pl.ds(Y0, NY))
     local = [
         pltpu.make_async_copy(flags, FL.at[own], lsem.at[0]),
         pltpu.make_async_copy(press, PR.at[pl.ds(1, NX), pl.ds(Y0, NY)], lsem.at[1]),
-        pltpu.make_async_copy(vel, VEL.at[:, :, pl.ds(Y0, NY)], lsem.at[2]),
+        pltpu.make_async_copy(vel, VEL, lsem.at[2]),
         pltpu.make_async_copy(visc, VI.at[own], lsem.at[3]),
     ]
     for copy in local:
@@ -90,37 +96,60 @@
     PR[0] = jnp.zeros((EY, NZ), F32)
     PR[1:, 0:Y0] = jnp.zeros((NX, Y0, NZ), F32)
     PR[1:, Y1:EY] = jnp.zeros((NX, EY - Y1, NZ), F32)
-    RAWIN[...] = jnp.zeros((1, EY, NZ), F32)
+    RAWIN[...] = jnp.zeros((1, NY, NZ), F32)
     for c in range(3):
         V2[c, X1] = jnp.zeros((EY, NZ), F32)
-        VEL[c, :, 0:Y0] = jnp.zeros((NX, Y0, NZ), F32)
-        VEL[c, :, Y1:EY] = jnp.zeros((NX, EY - Y1, NZ), F32)
 
     barrier = pltpu.get_barrier_semaphore()
 
     def greet(device):
         pl.semaphore_signal(barrier, inc=1, device_id=device, device_id_type=MESH)
 
-    near = [(has_xlo, xlo), (has_xhi, xhi), (has_ylo, ylo), (has_yhi, yhi)]
+    far_up = (py == 3) & has_xhi
+    relay = (py == 2) & (gx < gxn - 2)
+    far_down = (py == 0) & has_xlo
+    near = [
+        (has_xlo, xlo), (has_xhi, xhi), (has_ylo, ylo), (has_yhi, yhi),
+        (relay, (gx + 2, gy)), (far_down, (gx - 2, gy)),
+    ]
     for there, device in near:
         pl.when(there)(lambda device=device: greet(device))
 
-    @pl.loop(1, CARD)
-    def _(d):
-        greet(card_device(lax.rem(card + d, CARD)))
-
-    @pl.loop(1, RING)
-    def _(d):
-        greet(ring_device(lax.rem(ring + d, RING)))
+    for device in ring_peers + card_peers:
+        greet(device)
+
+    def is_fluid(f):
+        return jnp.where(f == 1, 1.0, 0.0)
+
+    def is_open(f):
+        return jnp.where(f != 0, 1.0, 0.0)
+
+    def pressed(a, b, y):
+        f = FL[a:b, y : y + NY]
+        fluid = is_fluid(f)
+        return fluid, is_open(f), PR[a - LOW + 1 : b - LOW + 1, y : y + NY] * fluid
+
+    for copy in local[:3]:
+        copy.wait()
+    for a, b in blocks(X0, X1, 2):
+        fluid, opened, p = pressed(a, b, Y0)
+        act = jnp.maximum(fluid, low_z(fluid)) * opened * low_z(opened)
+        S[2, a:b, Y0:Y1] = act * (VEL[2, a - X0 : b - X0] - (p - low_z(p)))
+        if a == X0:
+            RAW[...] = VEL[0, 0:1] - p[0:1]
+            fluid, opened, p, a = fluid[1:], opened[1:], p[1:], a + 1
+        fluid_low, opened_low, p_low = pressed(a - 1, b - 1, Y0)
+        act = jnp.maximum(fluid, fluid_low) * opened * opened_low
+        S[0, a:b, Y0:Y1] = act * (VEL[0, a - X0 : b - X0] - (p - p_low))
 
     one = lambda there: jnp.where(there, 1, 0)
     pl.semaphore_wait(barrier, CARD + RING - 2 + sum(one(t) for t, _ in near))
 
     sent = []
 
-    def send(source, target, sems, n, to, there, from_):
+    def send(source, target, sems, n, to, there, from_, out=None):
         copy = pltpu.make_async_remote_copy(
-            src_ref=source, dst_ref=target, send_sem=sems[0].at[n], recv_sem=sems[1].at[n],
+            src_ref=source, dst_ref=target, send_sem=sems[0].at[n if out is None else out], recv_sem=sems[1].at[n],
             device_id=to, device_id_type=MESH,
         )
         pl.when(there)(copy.start)
@@ -137,67 +166,66 @@
     ylast, yfirst = pl.ds(NY - LOW, LOW), pl.ds(0, HIGH)
     elast, efirst = pl.ds(Y1 - LOW, LOW), pl.ds(Y0, HIGH)
 
-    x_cells = [
-        send(flags.at[last4], FL.at[xlow, rows], X, 0, *UP),
-        send(flags.at[first3], FL.at[xhigh, rows], X, 1, *DOWN),
-        send(visc.at[last4], VI.at[xlow, rows], X, 2, *UP),
-        send(visc.at[first3], VI.at[xhigh, rows], X, 3, *DOWN),
-    ]
-    x_press = send(press.at[pl.ds(NX - 1, 1)], PR.at[pl.ds(0, 1), rows], X, 4, *UP)
+    u, v, w = 0, 1, 2
+    upper = pl.ds(X0 + 1, NX - 1)
+    top4, low3 = pl.ds(X1 - LOW, LOW), pl.ds(X0, HIGH)
+    far_cells = [
+        send(source.at[last4], target, X, n, xlo, far_up, relay)
+        for n, source, target in ((9, visc, VIA), (10, flags, FLA))
+    ]
+    direct_up = has_xhi & (py != 3)
+    x_started = [
+        send(S.at[u, top4, rows], S.at[u, xlow, rows], X, 5, *UP),
+        send(S.at[w, top4, rows], S.at[w, xlow, rows], X, 6, *UP),
+        send(RAW, RAWIN, X, 8, *DOWN),
+        send(S.at[u, pl.ds(X0 + 1, HIGH - 1), rows], S.at[u, pl.ds(X1 + 1, HIGH - 1), rows], X, 7, *DOWN),
+        send(S.at[w, low3, rows], S.at[w, xhigh, rows], X, 11, *DOWN),
+    ]
     y_press = send(press.at[:, pl.ds(NY - 1, 1)], PR.at[pl.ds(1, NX), pl.ds(Y0 - 1, 1)], Y, 0, *NORTH)
     y_flags = send(flags.at[:, ylast], FL.at[xown, ylow], Y, 1, *NORTH)
+    x_flags = send(flags.at[first3], FL.at[xhigh, rows], X, 1, *DOWN)
+    x_visc = send(visc.at[first3], VI.at[xhigh, rows], X, 3, *DOWN)
+    x_press = send(press.at[pl.ds(NX - 1, 1)], PR.at[pl.ds(0, 1), rows], X, 4, *UP)
+    x_cells = [
+        send(flags.at[last4], FL.at[xlow, rows], X, 0, xhi, direct_up, has_xlo),
+        x_flags,
+        send(visc.at[last4], VI.at[xlow, rows], X, 2, xhi, direct_up, has_xlo),
+        x_visc,
+    ]
     y_cells = [
         send(flags.at[:, yfirst], FL.at[xown, yhigh], Y, 2, *SOUTH),
         send(visc.at[:, ylast], VI.at[xown, ylow], Y, 3, *NORTH),
         send(visc.at[:, yfirst], VI.at[xown, yhigh], Y, 4, *SOUTH),
     ]
-
-    for copy in local[:3]:
-        copy.wait()
+    y_started = [
+        send(S.at[w, xown, elast], S.at[w, xown, ylow], Y, 5, *NORTH),
+        send(S.at[u, upper, elast], S.at[u, upper, ylow], Y, 6, *NORTH),
+        send(S.at[w, xown, efirst], S.at[w, xown, yhigh], Y, 7, *SOUTH),
+        send(S.at[u, upper, efirst], S.at[u, upper, yhigh], Y, 8, *SOUTH),
+    ]
+
     y_press()
     y_flags()
-    y_cells.pop(0)()
-
-    def is_fluid(f):
-        return jnp.where(f == 1, 1.0, 0.0)
-
-    def is_open(f):
-        return jnp.where(f != 0, 1.0, 0.0)
-
-    for a, b in blocks(X0, X1, 4):
-        f = FL[a:b]
-        fluid, opened = is_fluid(f), is_open(f)
-        p = PR[a - LOW + 1 : b - LOW + 1] * fluid
-        act = jnp.maximum(fluid, low_y(fluid)) * opened * low_y(opened)
-        S[1, a:b, Y0:Y1] = (act * (VEL[1, a - X0 : b - X0] - (p - low_y(p))))[:, Y0:Y1]
-        act = jnp.maximum(fluid, low_z(fluid)) * opened * low_z(opened)
-        S[2, a:b, Y0:Y1] = (act * (VEL[2, a - X0 : b - X0] - (p - low_z(p))))[:, Y0:Y1]
-        if a == X0:
-            RAW[...] = VEL[0, 0:1] - p[0:1]
-            fluid, opened, p, a = fluid[1:], opened[1:], p[1:], a + 1
-        below = FL[a - 1 : b - 1]
-        fluid_below = is_fluid(below)
-        p_below = PR[a - LOW : b - LOW] * fluid_below
-        act = jnp.maximum(fluid, fluid_below) * opened * is_open(below)
-        S[0, a:b, Y0:Y1] = (act * (VEL[0, a - X0 : b - X0] - (p - p_below)))[:, Y0:Y1]
-
-    vw = pl.ds(1, 2)
-    x_started = [
-        send(S.at[:, pl.ds(X1 - LOW, LOW), rows], S.at[:, xlow, rows], X, 5, *UP),
-        send(S.at[vw, pl.ds(X0, HIGH), rows], S.at[vw, xhigh, rows], X, 6, *DOWN),
-        send(S.at[0, pl.ds(X0 + 1, HIGH - 1), rows], S.at[0, pl.ds(X1 + 1, HIGH - 1), rows], X, 7, *DOWN),
-        send(RAW.at[:, rows], RAWIN.at[:, rows], X, 8, *DOWN),
-    ]
-    upper = pl.ds(X0 + 1, NX - 1)
-    y_started = [
-        send(S.at[vw, xown, elast], S.at[vw, xown, ylow], Y, 5, *NORTH),
-        send(S.at[0, upper, elast], S.at[0, upper, ylow], Y, 6, *NORTH),
-        send(S.at[vw, xown, efirst], S.at[vw, xown, yhigh], Y, 7, *SOUTH),
-        send(S.at[0, upper, efirst], S.at[0, upper, yhigh], Y, 8, *SOUTH),
-    ]
+    for a, b in blocks(X0, X1, 2):
+        fluid, opened, p = pressed(a, b, Y0)
+        fluid_low, opened_low, p_low = pressed(a, b, Y0 - 1)
+        act = jnp.maximum(fluid, fluid_low) * opened * opened_low
+        S[1, a:b, Y0:Y1] = act * (VEL[1, a - X0 : b - X0] - (p - p_low))
+    x_started += [
+        send(S.at[v, top4, rows], S.at[v, xlow, rows], X, 12, *UP),
+        send(S.at[v, low3, rows], S.at[v, xhigh, rows], X, 13, *DOWN),
+    ]
+    y_started += [
+        send(S.at[v, xown, elast], S.at[v, xown, ylow], Y, 9, *NORTH),
+        send(S.at[v, xown, efirst], S.at[v, xown, yhigh], Y, 10, *SOUTH),
+    ]
+    for wait in far_cells:
+        wait()
+    for n, source, target in ((2, VIA, VI), (0, FLA, FL)):
+        send(source, target.at[xlow, rows], X, n, (gx + 2, gy), relay, None, out=14 + n // 2)
 
     local[3].wait()
-    n = 9
+    n = 11
     for wait in x_cells:
         wait()
     for ref in (FL, VI):
@@ -240,10 +268,10 @@
     for wait in x_started:
         wait()
     x_press()
-    for layer, below, raw in ((X0, PR[0:1], RAW[...]), (X1, PR[NX : NX + 1], RAWIN[...])):
-        f, g = FL[layer : layer + 1], FL[layer - 1 : layer]
+    for layer, below, raw in ((X0, 0, RAW), (X1, NX, RAWIN)):
+        f, g = FL[layer : layer + 1, Y0:Y1], FL[layer - 1 : layer, Y0:Y1]
         act = jnp.maximum(is_fluid(f), is_fluid(g)) * is_open(f) * is_open(g)
-        S[0, layer : layer + 1, Y0:Y1] = (act * (raw + below * is_fluid(g)))[:, Y0:Y1]
+        S[0, layer : layer + 1, Y0:Y1] = act * (raw[...] + PR[below : below + 1, Y0:Y1] * is_fluid(g))
     lowest = pl.ds(X0, 1)
     for there, at in ((S, (slice(None), xlow)), (S, (slice(None), xhigh)), (S, (0, lowest))):
         y_started.append(send(there.at[(*at, elast)], there.at[(*at, ylow)], Y, n, *NORTH))
@@ -338,37 +366,26 @@
         total = jnp.sum(jnp.sum(value[0], axis=0, keepdims=True), axis=1, keepdims=True)
         payload = jnp.where(lane == k, total, payload)
 
-    def gather(slots, count, me, device, sends, recvs, value):
+    def gather(slots, me, peers, n, value):
         slots[me] = value
-        copy = lambda peer: pltpu.make_async_remote_copy(
-            src_ref=slots.at[me], dst_ref=slots.at[me], send_sem=sends.at[peer], recv_sem=recvs.at[me],
-            device_id=device(peer), device_id_type=MESH,
+        for device in peers:
+            pltpu.make_async_remote_copy(
+                src_ref=slots.at[me], dst_ref=slots.at[me], send_sem=gs.at[n], recv_sem=gr.at[n],
+                device_id=device, device_id_type=MESH,
+            ).start()
+        rest = slots.at[pl.ds(0, len(peers))]
+        every = pltpu.make_async_remote_copy(
+            src_ref=rest, dst_ref=rest, send_sem=gs.at[n], recv_sem=gr.at[n],
+            device_id=peers[0], device_id_type=MESH,
         )
-        arrival = lambda peer: pltpu.make_async_remote_copy(
-            src_ref=slots.at[me], dst_ref=slots.at[peer], send_sem=sends.at[peer], recv_sem=recvs.at[peer],
-            device_id=device(peer), device_id_type=MESH,
-        )
-
-        @pl.loop(1, count)
-        def _(d):
-            copy(lax.rem(me + d, count)).start()
-
-        @pl.loop(1, count)
-        def _(d):
-            arrival(lax.rem(me + d, count)).wait_recv()
-
-        def finish():
-            @pl.loop(1, count)
-            def _(d):
-                copy(lax.rem(me + d, count)).wait_send()
-
+        every.wait_recv()
         total = slots[0]
-        for r in range(1, count):
+        for r in range(1, len(peers) + 1):
             total = total + slots[r]
-        return total, finish
-
-    total, finish_cards = gather(CARDS, CARD, card, card_device, cs, cr, payload)
-    total, finish_rings = gather(RINGS, RING, ring, ring_device, rs, rr, total)
+        return total, every.wait_send
+
+    total, finish_cards = gather(CARDS, card, card_peers, 0, payload)
+    total, finish_rings = gather(RINGS, ring, ring_peers, 1, total)
 
     wide = jnp.broadcast_to(total, (8, NZ))
     at = lax.broadcasted_iota(jnp.int32, (8, NZ), 1)
@@ -426,14 +443,15 @@
             in_specs=[pl.BlockSpec(memory_space=pl.ANY)] * 4,
             out_specs=pl.BlockSpec(memory_space=pltpu.VMEM),
             scratch_shapes=[
-                *[field(3, *ext)] * 4, field(3, NX, EY, NZ), field(*ext), pltpu.VMEM(ext, jnp.int32),
-                field(NX + 1, EY, NZ), field(1, EY, NZ), field(1, EY, NZ),
+                *[field(3, *ext)] * 4, field(3, NX, NY, NZ), field(*ext), pltpu.VMEM(ext, jnp.int32),
+                field(NX + 1, EY, NZ), field(1, NY, NZ), field(1, NY, NZ),
+                field(LOW, NY, NZ), pltpu.VMEM((LOW, NY, NZ), jnp.int32),
                 *[field(*ext)] * 9,
                 field(CARD, 1, NZ), field(RING, 1, NZ),
-                dma(4), dma(9), dma(9), dma(23), dma(23), dma(CARD), dma(CARD), dma(RING), dma(RING),
+                dma(4), dma(16), dma(14), dma(25), dma(25), dma(2), dma(2),
             ],
             compiler_params=pltpu.CompilerParams(
-                collective_id=1, has_side_effects=True, vmem_limit_bytes=48 * 2**20
+                collective_id=1, has_side_effects=True, vmem_limit_bytes=60 * 2**20
             ),
         )(velocity, viscosity, pressure, flags)
 

time: 62.3 us -> 57.1 us (0.917)
  Pallas kernels: 57.9 us -> 55.4 us
  local copies, waits for them, and re-layouts: 4.12 us -> 1.62 us
    unnamed x9 -> x1, local copies, waits for them, and re-layouts: 4.12 us -> 1.62 us
    pallas_call x1, Pallas kernels: 57.9 us -> 55.4 us  [local(): pl.pallas_call(body, out_shape=jax.ShapeDtypeStruct((3, NX, NY, NZ), F32)...]
where the time goes in v2:
time: 57.1 us; the launch traced here: 57 us
  Pallas kernels  55.4 us (97%)
  local copies, waits for them, and re-layouts  1.62 us (3%)
    pallas_call x1, Pallas kernels, local(): pl.pallas_call(body, out_shape=jax.ShapeDtypeStruct((3, NX, NY, NZ), F32)...  55.4 us
    unnamed x1, local copies, waits for them, and re-layouts  1.62 us

profile of v2, /device:TPU:1, one launch (start us, length us, event | category | flops | bytes accessed | tf_op | source)
XLA Modules:
  0.0 57.0 jit_solution(6078799437143397533)
XLA Ops:
  0.0 55.4 %shard_map.46 = f32[3,8,16,128]{3,2,1,0:T(8,128)} custom-call(f32[3,8,16,128]{3,2,1,0:T(8,128)} %refs_0_.1, f32[8,16,128]{2,1,0:T(8,128)} %refs_1_.1, f32[8,16,128]{2,1,0:T(8,128)} %refs_2_.1, s32[8,16,128]{2,1,0:T(8,128)} %refs_3_.1), custom_call_target="tpu_custom_call" | custom-call | tf_op jit(solution)/shard_map/pallas_call | solution.py:440
  55.4 1.6 %copy.6 = f32[3,8,16,128]{3,2,1,0:T(8,128)} copy(f32[3,8,16,128]{3,2,1,0:T(8,128)} %shard_map.46) | data formatting | bytes 393216

commit v3 on v2

--- a/solution.py
+++ b/solution.py
@@ -44,7 +44,7 @@
 def kernel(
     gxn, gyn,
     vel, visc, press, flags, out,
-    S, V0, V1, V2, VEL, VI, FL, PR, RAW, RAWIN, VIA, FLA,
+    S, V0, V1, V2, VEL, VI, FL, PR, RAW, RAWIN, VIA, FLA, PRA, VIB, FLB,
     CW, WXY, WXZ, WYZ, EU, EV, DU, DV, DW,
     CARDS, RINGS,
     lsem, xs, xr, ys, yr, gs, gr,
@@ -105,12 +105,11 @@
     def greet(device):
         pl.semaphore_signal(barrier, inc=1, device_id=device, device_id_type=MESH)
 
-    far_up = (py == 3) & has_xhi
-    relay = (py == 2) & (gx < gxn - 2)
-    far_down = (py == 0) & has_xlo
+    far_up, far_down = (py == 3) & has_xhi, (py == 0) & has_xlo
+    pass_up, pass_down = (py == 2) & (gx < gxn - 2), (py == 1) & (gx >= 2)
     near = [
-        (has_xlo, xlo), (has_xhi, xhi), (has_ylo, ylo), (has_yhi, yhi),
-        (relay, (gx + 2, gy)), (far_down, (gx - 2, gy)),
+        (far_up, xhi), (far_down, xlo), (pass_up | far_up, (gx + 2, gy)), (pass_down | far_down, (gx - 2, gy)),
+        (has_xlo & (py != 0), xlo), (has_xhi & (py != 3), xhi), (has_ylo, ylo), (has_yhi, yhi),
     ]
     for there, device in near:
         pl.when(there)(lambda device=device: greet(device))
@@ -169,11 +168,13 @@
     u, v, w = 0, 1, 2
     upper = pl.ds(X0 + 1, NX - 1)
     top4, low3 = pl.ds(X1 - LOW, LOW), pl.ds(X0, HIGH)
-    far_cells = [
-        send(source.at[last4], target, X, n, xlo, far_up, relay)
-        for n, source, target in ((9, visc, VIA), (10, flags, FLA))
-    ]
-    direct_up = has_xhi & (py != 3)
+    passing = [
+        (visc.at[last4], VIA, VI.at[xlow, rows], 2), (flags.at[last4], FLA, FL.at[xlow, rows], 0),
+        (press.at[pl.ds(NX - 1, 1)], PRA, PR.at[pl.ds(0, 1), rows], 4),
+    ], [(visc.at[first3], VIB, VI.at[xhigh, rows], 3), (flags.at[first3], FLB, FL.at[xhigh, rows], 1)]
+    far_cells = [send(part[0], part[1], X, 14 + k, xlo, far_up, pass_up) for k, part in enumerate(passing[0])]
+    far_cells += [send(part[0], part[1], X, 17 + k, xhi, far_down, pass_down) for k, part in enumerate(passing[1])]
+    direct_up, direct_down = (xhi, has_xhi & (py != 3), has_xlo), (xlo, has_xlo & (py != 0), has_xhi)
     x_started = [
         send(S.at[u, top4, rows], S.at[u, xlow, rows], X, 5, *UP),
         send(S.at[w, top4, rows], S.at[w, xlow, rows], X, 6, *UP),
@@ -183,13 +184,13 @@
     ]
     y_press = send(press.at[:, pl.ds(NY - 1, 1)], PR.at[pl.ds(1, NX), pl.ds(Y0 - 1, 1)], Y, 0, *NORTH)
     y_flags = send(flags.at[:, ylast], FL.at[xown, ylow], Y, 1, *NORTH)
-    x_flags = send(flags.at[first3], FL.at[xhigh, rows], X, 1, *DOWN)
-    x_visc = send(visc.at[first3], VI.at[xhigh, rows], X, 3, *DOWN)
-    x_press = send(press.at[pl.ds(NX - 1, 1)], PR.at[pl.ds(0, 1), rows], X, 4, *UP)
+    x_flags = send(flags.at[first3], FL.at[xhigh, rows], X, 1, *direct_down)
+    x_visc = send(visc.at[first3], VI.at[xhigh, rows], X, 3, *direct_down)
+    x_press = send(press.at[pl.ds(NX - 1, 1)], PR.at[pl.ds(0, 1), rows], X, 4, *direct_up)
     x_cells = [
-        send(flags.at[last4], FL.at[xlow, rows], X, 0, xhi, direct_up, has_xlo),
+        send(flags.at[last4], FL.at[xlow, rows], X, 0, *direct_up),
         x_flags,
-        send(visc.at[last4], VI.at[xlow, rows], X, 2, xhi, direct_up, has_xlo),
+        send(visc.at[last4], VI.at[xlow, rows], X, 2, *direct_up),
         x_visc,
     ]
     y_cells = [
@@ -221,8 +222,10 @@
     ]
     for wait in far_cells:
         wait()
-    for n, source, target in ((2, VIA, VI), (0, FLA, FL)):
-        send(source, target.at[xlow, rows], X, n, (gx + 2, gy), relay, None, out=14 + n // 2)
+    for _, source, target, n in passing[0]:
+        send(source, target, X, n, (gx + 2, gy), pass_up, None, out=19 + n)
+    for _, source, target, n in passing[1]:
+        send(source, target, X, n, (gx - 2, gy), pass_down, None, out=19 + n)
 
     local[3].wait()
     n = 11
@@ -445,14 +448,15 @@
             scratch_shapes=[
                 *[field(3, *ext)] * 4, field(3, NX, NY, NZ), field(*ext), pltpu.VMEM(ext, jnp.int32),
                 field(NX + 1, EY, NZ), field(1, NY, NZ), field(1, NY, NZ),
-                field(LOW, NY, NZ), pltpu.VMEM((LOW, NY, NZ), jnp.int32),
+                field(LOW, NY, NZ), pltpu.VMEM((LOW, NY, NZ), jnp.int32), field(1, NY, NZ),
+                field(HIGH, NY, NZ), pltpu.VMEM((HIGH, NY, NZ), jnp.int32),
                 *[field(*ext)] * 9,
                 field(CARD, 1, NZ), field(RING, 1, NZ),
-                dma(4), dma(16), dma(14), dma(25), dma(25), dma(2), dma(2),
+                dma(4), dma(24), dma(19), dma(25), dma(25), dma(2), dma(2),
             ],
             compiler_params=pltpu.CompilerParams(
-                collective_id=1, has_side_effects=True, vmem_limit_bytes=60 * 2**20
+                collective_id=1, has_side_effects=True, vmem_limit_bytes=48 * 2**20
             ),
-        )(velocity, viscosity, pressure, flags)
+        )(*[pltpu.with_memory_space_constraint(a, pltpu.HBM) for a in (velocity, viscosity, pressure, flags)])
 
     return jax.shard_map(local, mesh=mesh, in_specs=(block, cells, cells, cells), out_specs=block, check_vma=False)

time: 57.1 us -> 53.1 us (0.930)
  Pallas kernels: 55.4 us -> 52.3 us
  local copies, waits for them, and re-layouts: 1.62 us -> 0.68 us
    pallas_call x1, Pallas kernels: 55.4 us -> 52.3 us  [local(): pl.pallas_call(body, out_shape=jax.ShapeDtypeStruct((3, NX, NY, NZ), F32)...]
    unnamed x1, local copies, waits for them, and re-layouts: 1.62 us -> 0.68 us
where the time goes in v3:
time: 53.1 us; the launch traced here: 53 us
  Pallas kernels  52.3 us (98%)
  local copies, waits for them, and re-layouts  0.68 us (1%)
    pallas_call x1, Pallas kernels, local(): pl.pallas_call(body, out_shape=jax.ShapeDtypeStruct((3, NX, NY, NZ), F32)...  52.3 us

profile of v3, /device:TPU:1, one launch (start us, length us, event | category | flops | bytes accessed | tf_op | source)
XLA Modules:
  0.0 53.0 jit_solution(7384111675001162505)
XLA Ops:
  0.0 52.3 %shard_map.46 = f32[3,8,16,128]{3,2,1,0:T(8,128)S(1)} custom-call(f32[3,8,16,128]{3,2,1,0:T(8,128)} %refs_0_.1, f32[8,16,128]{2,1,0:T(8,128)} %refs_1_.1, f32[8,16,128]{2,1,0:T(8,128)} %refs_2_.1, s32[8,16,128]{2,1,0:T(8,128)} %refs_3_.1), custom_call_target="tpu_custom_call" | custom-call | tf_op jit(solution)/shard_map/pallas_call | solution.py:443
  52.3 0.7 %copy.6 = f32[3,8,16,128]{3,2,1,0:T(8,128)} copy(f32[3,8,16,128]{3,2,1,0:T(8,128)S(1)} %shard_map.46) | data formatting | bytes 393216

commit v4 on v3

--- a/solution.py
+++ b/solution.py
@@ -44,7 +44,7 @@
 def kernel(
     gxn, gyn,
     vel, visc, press, flags, out,
-    S, V0, V1, V2, VEL, VI, FL, PR, RAW, RAWIN, VIA, FLA, PRA, VIB, FLB,
+    S, V0, V1, V2, VEL, VI, FL, PR, RAW, RAWIN, VIA, FLA, VIB,
     CW, WXY, WXZ, WYZ, EU, EV, DU, DV, DW,
     CARDS, RINGS,
     lsem, xs, xr, ys, yr, gs, gr,
@@ -81,24 +81,18 @@
     for copy in local:
         copy.start()
 
-    def clear(ref, lead, kind):
-        zero = lambda *shape: jnp.zeros(shape, kind)
-        for c in range(lead) if lead else [None]:
-            at = ref if c is None else ref.at[c]
-            at[0:X0] = zero(X0, EY, NZ)
-            at[X1:EX] = zero(EX - X1, EY, NZ)
-            at[X0:X1, 0:Y0] = zero(NX, Y0, NZ)
-            at[X0:X1, Y1:EY] = zero(NX, EY - Y1, NZ)
-
-    clear(S, 3, F32)
-    clear(VI, 0, F32)
-    clear(FL, 0, jnp.int32)
-    PR[0] = jnp.zeros((EY, NZ), F32)
-    PR[1:, 0:Y0] = jnp.zeros((NX, Y0, NZ), F32)
-    PR[1:, Y1:EY] = jnp.zeros((NX, EY - Y1, NZ), F32)
-    RAWIN[...] = jnp.zeros((1, NY, NZ), F32)
-    for c in range(3):
-        V2[c, X1] = jnp.zeros((EY, NZ), F32)
+    @pl.when((gx == 0) | (gx == gxn - 1) | (gy == 0) | (gy == gyn - 1))
+    def _():
+        for ref in (S.at[0], S.at[1], S.at[2], VI, FL):
+            ref[0:X0] = jnp.zeros((X0, EY, NZ), ref.dtype)
+            ref[X1:EX] = jnp.zeros((EX - X1, EY, NZ), ref.dtype)
+            ref[X0:X1, 0:Y0] = jnp.zeros((NX, Y0, NZ), ref.dtype)
+            ref[X0:X1, Y1:EY] = jnp.zeros((NX, EY - Y1, NZ), ref.dtype)
+        PR[0] = jnp.zeros((EY, NZ), F32)
+        PR[1:, 0:Y0] = jnp.zeros((NX, Y0, NZ), F32)
+        RAWIN[...] = jnp.zeros((1, NY, NZ), F32)
+        for c in range(3):
+            V2[c, X1] = jnp.zeros((EY, NZ), F32)
 
     barrier = pltpu.get_barrier_semaphore()
 
@@ -146,12 +140,15 @@
 
     sent = []
 
-    def send(source, target, sems, n, to, there, from_, out=None):
+    def send(source, target, sems, n, to, there, from_, out=None, later=None):
         copy = pltpu.make_async_remote_copy(
             src_ref=source, dst_ref=target, send_sem=sems[0].at[n if out is None else out], recv_sem=sems[1].at[n],
             device_id=to, device_id_type=MESH,
         )
-        pl.when(there)(copy.start)
+        if later is None:
+            pl.when(there)(copy.start)
+        else:
+            later.append((there, copy))
         sent.append((there, copy))
         return lambda: pl.when(from_)(copy.wait_recv)
 
@@ -165,34 +162,45 @@
     ylast, yfirst = pl.ds(NY - LOW, LOW), pl.ds(0, HIGH)
     elast, efirst = pl.ds(Y1 - LOW, LOW), pl.ds(Y0, HIGH)
 
+    def start(up, down, far):
+        for copies, crosses in ((up, py == 3), (down, py == 0)):
+            for there, copy in copies:
+                pl.when(there & (crosses if far else jnp.logical_not(crosses)))(copy.start)
+
+    up, down = [], []
+    y_press = send(press.at[:, pl.ds(NY - 1, 1)], PR.at[pl.ds(1, NX), pl.ds(Y0 - 1, 1)], Y, 0, *NORTH)
+    y_flags = send(flags.at[:, ylast], FL.at[xown, ylow], Y, 1, *NORTH)
     u, v, w = 0, 1, 2
     upper = pl.ds(X0 + 1, NX - 1)
     top4, low3 = pl.ds(X1 - LOW, LOW), pl.ds(X0, HIGH)
+    half = LOW // 2
     passing = [
-        (visc.at[last4], VIA, VI.at[xlow, rows], 2), (flags.at[last4], FLA, FL.at[xlow, rows], 0),
-        (press.at[pl.ds(NX - 1, 1)], PRA, PR.at[pl.ds(0, 1), rows], 4),
-    ], [(visc.at[first3], VIB, VI.at[xhigh, rows], 3), (flags.at[first3], FLB, FL.at[xhigh, rows], 1)]
+        (visc.at[last4], VIA, VI.at[xlow, rows], 2),
+        (flags.at[pl.ds(NX - LOW, half)], FLA, FL.at[pl.ds(0, half), rows], 0),
+    ], [(visc.at[first3], VIB, VI.at[xhigh, rows], 3)]
     far_cells = [send(part[0], part[1], X, 14 + k, xlo, far_up, pass_up) for k, part in enumerate(passing[0])]
     far_cells += [send(part[0], part[1], X, 17 + k, xhi, far_down, pass_down) for k, part in enumerate(passing[1])]
     direct_up, direct_down = (xhi, has_xhi & (py != 3), has_xlo), (xlo, has_xlo & (py != 0), has_xhi)
     x_started = [
-        send(S.at[u, top4, rows], S.at[u, xlow, rows], X, 5, *UP),
-        send(S.at[w, top4, rows], S.at[w, xlow, rows], X, 6, *UP),
-        send(RAW, RAWIN, X, 8, *DOWN),
-        send(S.at[u, pl.ds(X0 + 1, HIGH - 1), rows], S.at[u, pl.ds(X1 + 1, HIGH - 1), rows], X, 7, *DOWN),
-        send(S.at[w, low3, rows], S.at[w, xhigh, rows], X, 11, *DOWN),
-    ]
-    y_press = send(press.at[:, pl.ds(NY - 1, 1)], PR.at[pl.ds(1, NX), pl.ds(Y0 - 1, 1)], Y, 0, *NORTH)
-    y_flags = send(flags.at[:, ylast], FL.at[xown, ylow], Y, 1, *NORTH)
-    x_flags = send(flags.at[first3], FL.at[xhigh, rows], X, 1, *direct_down)
-    x_visc = send(visc.at[first3], VI.at[xhigh, rows], X, 3, *direct_down)
-    x_press = send(press.at[pl.ds(NX - 1, 1)], PR.at[pl.ds(0, 1), rows], X, 4, *direct_up)
+        send(S.at[u, top4, rows], S.at[u, xlow, rows], X, 5, *UP, later=up),
+        send(S.at[w, top4, rows], S.at[w, xlow, rows], X, 6, *UP, later=up),
+        send(RAW, RAWIN, X, 8, *DOWN, later=down),
+        send(S.at[u, pl.ds(X0 + 1, HIGH - 1), rows], S.at[u, pl.ds(X1 + 1, HIGH - 1), rows], X, 7, *DOWN, later=down),
+        send(S.at[w, low3, rows], S.at[w, xhigh, rows], X, 11, *DOWN, later=down),
+    ]
     x_cells = [
-        send(flags.at[last4], FL.at[xlow, rows], X, 0, *direct_up),
-        x_flags,
-        send(visc.at[last4], VI.at[xlow, rows], X, 2, *direct_up),
-        x_visc,
-    ]
+        send(flags.at[first3], FL.at[xhigh, rows], X, 1, *DOWN, later=down),
+        send(flags.at[pl.ds(NX - half, half)], FL.at[pl.ds(half, half), rows], X, 16, *UP, later=up),
+    ]
+    x_press = send(press.at[pl.ds(NX - 1, 1)], PR.at[pl.ds(0, 1), rows], X, 4, *UP, later=up)
+    start(up, down, True)
+    x_cells += [
+        send(flags.at[pl.ds(NX - LOW, half)], FL.at[pl.ds(0, half), rows], X, 0, *direct_up, later=up),
+        send(visc.at[last4], VI.at[xlow, rows], X, 2, *direct_up, later=up),
+        send(visc.at[first3], VI.at[xhigh, rows], X, 3, *direct_down, later=down),
+    ]
+    near_up, near_down = up, down
+    up, down = [], []
     y_cells = [
         send(flags.at[:, yfirst], FL.at[xown, yhigh], Y, 2, *SOUTH),
         send(visc.at[:, ylast], VI.at[xown, ylow], Y, 3, *NORTH),
@@ -213,9 +221,10 @@
         act = jnp.maximum(fluid, fluid_low) * opened * opened_low
         S[1, a:b, Y0:Y1] = act * (VEL[1, a - X0 : b - X0] - (p - p_low))
     x_started += [
-        send(S.at[v, top4, rows], S.at[v, xlow, rows], X, 12, *UP),
-        send(S.at[v, low3, rows], S.at[v, xhigh, rows], X, 13, *DOWN),
-    ]
+        send(S.at[v, top4, rows], S.at[v, xlow, rows], X, 12, *UP, later=up),
+        send(S.at[v, low3, rows], S.at[v, xhigh, rows], X, 13, *DOWN, later=down),
+    ]
+    start(up, down, True)
     y_started += [
         send(S.at[v, xown, elast], S.at[v, xown, ylow], Y, 9, *NORTH),
         send(S.at[v, xown, efirst], S.at[v, xown, yhigh], Y, 10, *SOUTH),
@@ -226,6 +235,7 @@
         send(source, target, X, n, (gx + 2, gy), pass_up, None, out=19 + n)
     for _, source, target, n in passing[1]:
         send(source, target, X, n, (gx - 2, gy), pass_down, None, out=19 + n)
+    start(near_up + up, near_down + down, False)
 
     local[3].wait()
     n = 11
@@ -236,6 +246,18 @@
             y_cells.append(send(ref.at[layers, elast], ref.at[layers, ylow], Y, n, *NORTH))
             y_cells.append(send(ref.at[layers, efirst], ref.at[layers, yhigh], Y, n + 1, *SOUTH))
             n += 2
+    for wait in x_started:
+        wait()
+    x_press()
+    for layer, below, raw in ((X0, 0, RAW), (X1, NX, RAWIN)):
+        f, g = FL[layer : layer + 1, Y0:Y1], FL[layer - 1 : layer, Y0:Y1]
+        act = jnp.maximum(is_fluid(f), is_fluid(g)) * is_open(f) * is_open(g)
+        S[0, layer : layer + 1, Y0:Y1] = act * (raw[...] + PR[below : below + 1, Y0:Y1] * is_fluid(g))
+    lowest = pl.ds(X0, 1)
+    for there, at in ((S, (slice(None), xlow)), (S, (slice(None), xhigh)), (S, (0, lowest))):
+        y_started.append(send(there.at[(*at, elast)], there.at[(*at, ylow)], Y, n, *NORTH))
+        y_started.append(send(there.at[(*at, efirst)], there.at[(*at, yhigh)], Y, n + 1, *SOUTH))
+        n += 2
     for wait in y_cells:
         wait()
 
@@ -268,18 +290,6 @@
         act = jnp.maximum(fc, low_z(fc)) * oc * low_z(oc)
         DW[a:b] = act / (1.0 + cw + low_z(cw) + xz + wxz[1:] + wyz + next_y(wyz))
 
-    for wait in x_started:
-        wait()
-    x_press()
-    for layer, below, raw in ((X0, 0, RAW), (X1, NX, RAWIN)):
-        f, g = FL[layer : layer + 1, Y0:Y1], FL[layer - 1 : layer, Y0:Y1]
-        act = jnp.maximum(is_fluid(f), is_fluid(g)) * is_open(f) * is_open(g)
-        S[0, layer : layer + 1, Y0:Y1] = act * (raw[...] + PR[below : below + 1, Y0:Y1] * is_fluid(g))
-    lowest = pl.ds(X0, 1)
-    for there, at in ((S, (slice(None), xlow)), (S, (slice(None), xhigh)), (S, (0, lowest))):
-        y_started.append(send(there.at[(*at, elast)], there.at[(*at, ylow)], Y, n, *NORTH))
-        y_started.append(send(there.at[(*at, efirst)], there.at[(*at, yhigh)], Y, n + 1, *SOUTH))
-        n += 2
     for wait in y_started:
         wait()
 
@@ -369,7 +379,7 @@
         total = jnp.sum(jnp.sum(value[0], axis=0, keepdims=True), axis=1, keepdims=True)
         payload = jnp.where(lane == k, total, payload)
 
-    def gather(slots, me, peers, n, value):
+    def gather(slots, me, peers, n, value, meanwhile):
         slots[me] = value
         for device in peers:
             pltpu.make_async_remote_copy(
@@ -381,14 +391,19 @@
             src_ref=rest, dst_ref=rest, send_sem=gs.at[n], recv_sem=gr.at[n],
             device_id=peers[0], device_id_type=MESH,
         )
+        meanwhile()
         every.wait_recv()
         total = slots[0]
         for r in range(1, len(peers) + 1):
             total = total + slots[r]
         return total, every.wait_send
 
-    total, finish_cards = gather(CARDS, card, card_peers, 0, payload)
-    total, finish_rings = gather(RINGS, ring, ring_peers, 1, total)
+    def finish_sent():
+        for there, copy in sent:
+            pl.when(there)(copy.wait_send)
+
+    total, finish_cards = gather(CARDS, card, card_peers, 0, payload, finish_sent)
+    total, finish_rings = gather(RINGS, ring, ring_peers, 1, total, finish_cards)
 
     wide = jnp.broadcast_to(total, (8, NZ))
     at = lax.broadcasted_iota(jnp.int32, (8, NZ), 1)
@@ -423,9 +438,6 @@
             out[c, a - X0 : b - X0] = (
                 S[c, a:b, Y0:Y1] + c0 * V0[c, a:b, Y0:Y1] + c1 * V1[c, a:b, Y0:Y1] + c2 * V2[c, a:b, Y0:Y1]
             )
-    for there, copy in sent:
-        pl.when(there)(copy.wait_send)
-    finish_cards()
     finish_rings()
 
 
@@ -448,8 +460,7 @@
             scratch_shapes=[
                 *[field(3, *ext)] * 4, field(3, NX, NY, NZ), field(*ext), pltpu.VMEM(ext, jnp.int32),
                 field(NX + 1, EY, NZ), field(1, NY, NZ), field(1, NY, NZ),
-                field(LOW, NY, NZ), pltpu.VMEM((LOW, NY, NZ), jnp.int32), field(1, NY, NZ),
-                field(HIGH, NY, NZ), pltpu.VMEM((HIGH, NY, NZ), jnp.int32),
+                field(LOW, NY, NZ), pltpu.VMEM((LOW // 2, NY, NZ), jnp.int32), field(HIGH, NY, NZ),
                 *[field(*ext)] * 9,
                 field(CARD, 1, NZ), field(RING, 1, NZ),
                 dma(4), dma(24), dma(19), dma(25), dma(25), dma(2), dma(2),

time: 53.1 us -> 51.6 us (0.972)
  Pallas kernels: 52.3 us -> 50.8 us
    pallas_call x1, Pallas kernels: 52.3 us -> 50.8 us  [local(): pl.pallas_call(body, out_shape=jax.ShapeDtypeStruct((3, NX, NY, NZ), F32)...]
where the time goes in v4:
time: 51.6 us; the launch traced here: 51.5 us
  Pallas kernels  50.8 us (98%)
  local copies, waits for them, and re-layouts  0.68 us (1%)
    pallas_call x1, Pallas kernels, local(): pl.pallas_call(body, out_shape=jax.ShapeDtypeStruct((3, NX, NY, NZ), F32)...  50.8 us

profile of v4, /device:TPU:1, one launch (start us, length us, event | category | flops | bytes accessed | tf_op | source)
XLA Modules:
  0.0 51.5 jit_solution(4812077361059486274)
XLA Ops:
  0.0 50.8 %shard_map.46 = f32[3,8,16,128]{3,2,1,0:T(8,128)S(1)} custom-call(f32[3,8,16,128]{3,2,1,0:T(8,128)} %refs_0_.1, f32[8,16,128]{2,1,0:T(8,128)} %refs_1_.1, f32[8,16,128]{2,1,0:T(8,128)} %refs_2_.1, s32[8,16,128]{2,1,0:T(8,128)} %refs_3_.1), custom_call_target="tpu_custom_call" | custom-call | tf_op jit(solution)/shard_map/pallas_call | solution.py:455
  50.8 0.7 %copy.6 = f32[3,8,16,128]{3,2,1,0:T(8,128)} copy(f32[3,8,16,128]{3,2,1,0:T(8,128)S(1)} %shard_map.46) | data formatting | bytes 393216

commit v5 on v4

--- a/solution.py
+++ b/solution.py
@@ -44,7 +44,7 @@
 def kernel(
     gxn, gyn,
     vel, visc, press, flags, out,
-    S, V0, V1, V2, VEL, VI, FL, PR, RAW, RAWIN, VIA, FLA, VIB,
+    S, V0, V1, V2, VEL, VI, FL, PR, RAW, RAWIN, VIA, FLA, VIB, FLB, PRA,
     CW, WXY, WXZ, WYZ, EU, EV, DU, DV, DW,
     CARDS, RINGS,
     lsem, xs, xr, ys, yr, gs, gr,
@@ -173,12 +173,14 @@
     u, v, w = 0, 1, 2
     upper = pl.ds(X0 + 1, NX - 1)
     top4, low3 = pl.ds(X1 - LOW, LOW), pl.ds(X0, HIGH)
-    half = LOW // 2
     passing = [
+        (flags.at[last4], FLA, FL.at[xlow, rows], 0),
         (visc.at[last4], VIA, VI.at[xlow, rows], 2),
-        (flags.at[pl.ds(NX - LOW, half)], FLA, FL.at[pl.ds(0, half), rows], 0),
-    ], [(visc.at[first3], VIB, VI.at[xhigh, rows], 3)]
-    far_cells = [send(part[0], part[1], X, 14 + k, xlo, far_up, pass_up) for k, part in enumerate(passing[0])]
+    ], [
+        (flags.at[first3], FLB, FL.at[xhigh, rows], 1),
+        (visc.at[first3], VIB, VI.at[xhigh, rows], 3),
+    ]
+    far_cells = [send(part[0], part[1], X, (9, 10, 14)[k], xlo, far_up, pass_up) for k, part in enumerate(passing[0])]
     far_cells += [send(part[0], part[1], X, 17 + k, xhi, far_down, pass_down) for k, part in enumerate(passing[1])]
     direct_up, direct_down = (xhi, has_xhi & (py != 3), has_xlo), (xlo, has_xlo & (py != 0), has_xhi)
     x_started = [
@@ -188,15 +190,12 @@
         send(S.at[u, pl.ds(X0 + 1, HIGH - 1), rows], S.at[u, pl.ds(X1 + 1, HIGH - 1), rows], X, 7, *DOWN, later=down),
         send(S.at[w, low3, rows], S.at[w, xhigh, rows], X, 11, *DOWN, later=down),
     ]
-    x_cells = [
-        send(flags.at[first3], FL.at[xhigh, rows], X, 1, *DOWN, later=down),
-        send(flags.at[pl.ds(NX - half, half)], FL.at[pl.ds(half, half), rows], X, 16, *UP, later=up),
-    ]
     x_press = send(press.at[pl.ds(NX - 1, 1)], PR.at[pl.ds(0, 1), rows], X, 4, *UP, later=up)
     start(up, down, True)
-    x_cells += [
-        send(flags.at[pl.ds(NX - LOW, half)], FL.at[pl.ds(0, half), rows], X, 0, *direct_up, later=up),
+    x_cells = [
+        send(flags.at[last4], FL.at[xlow, rows], X, 0, *direct_up, later=up),
         send(visc.at[last4], VI.at[xlow, rows], X, 2, *direct_up, later=up),
+        send(flags.at[first3], FL.at[xhigh, rows], X, 1, *direct_down, later=down),
         send(visc.at[first3], VI.at[xhigh, rows], X, 3, *direct_down, later=down),
     ]
     near_up, near_down = up, down
@@ -229,12 +228,10 @@
         send(S.at[v, xown, elast], S.at[v, xown, ylow], Y, 9, *NORTH),
         send(S.at[v, xown, efirst], S.at[v, xown, yhigh], Y, 10, *SOUTH),
     ]
-    for wait in far_cells:
+    for wait, (_, source, target, n) in zip(far_cells, passing[0] + passing[1]):
         wait()
-    for _, source, target, n in passing[0]:
-        send(source, target, X, n, (gx + 2, gy), pass_up, None, out=19 + n)
-    for _, source, target, n in passing[1]:
-        send(source, target, X, n, (gx - 2, gy), pass_down, None, out=19 + n)
+        to, there = ((gx + 2, gy), pass_up) if n % 2 == 0 else ((gx - 2, gy), pass_down)
+        send(source, target, X, n, to, there, None, out=19 + n)
     start(near_up + up, near_down + down, False)
 
     local[3].wait()
@@ -460,7 +457,8 @@
             scratch_shapes=[
                 *[field(3, *ext)] * 4, field(3, NX, NY, NZ), field(*ext), pltpu.VMEM(ext, jnp.int32),
                 field(NX + 1, EY, NZ), field(1, NY, NZ), field(1, NY, NZ),
-                field(LOW, NY, NZ), pltpu.VMEM((LOW // 2, NY, NZ), jnp.int32), field(HIGH, NY, NZ),
+                field(LOW, NY, NZ), pltpu.VMEM((LOW, NY, NZ), jnp.int32), field(HIGH, NY, NZ),
+                pltpu.VMEM((HIGH, NY, NZ), jnp.int32), field(1, NY, NZ),
                 *[field(*ext)] * 9,
                 field(CARD, 1, NZ), field(RING, 1, NZ),
                 dma(4), dma(24), dma(19), dma(25), dma(25), dma(2), dma(2),

time: 51.6 us -> 50.3 us (0.975)
  Pallas kernels: 50.8 us -> 49.5 us
    pallas_call x1, Pallas kernels: 50.8 us -> 49.5 us  [local(): pl.pallas_call(body, out_shape=jax.ShapeDtypeStruct((3, NX, NY, NZ), F32)...]
where the time goes in v5:
time: 50.3 us; the launch traced here: 50.2 us
  Pallas kernels  49.5 us (98%)
  local copies, waits for them, and re-layouts  0.68 us (1%)
    pallas_call x1, Pallas kernels, local(): pl.pallas_call(body, out_shape=jax.ShapeDtypeStruct((3, NX, NY, NZ), F32)...  49.5 us

profile of v5, /device:TPU:1, one launch (start us, length us, event | category | flops | bytes accessed | tf_op | source)
XLA Modules:
  0.0 50.2 jit_solution(17653997429281882228)
XLA Ops:
  0.0 49.5 %shard_map.46 = f32[3,8,16,128]{3,2,1,0:T(8,128)S(1)} custom-call(f32[3,8,16,128]{3,2,1,0:T(8,128)} %refs_0_.1, f32[8,16,128]{2,1,0:T(8,128)} %refs_1_.1, f32[8,16,128]{2,1,0:T(8,128)} %refs_2_.1, s32[8,16,128]{2,1,0:T(8,128)} %refs_3_.1), custom_call_target="tpu_custom_call" | custom-call | tf_op jit(solution)/shard_map/pallas_call | solution.py:452
  49.5 0.7 %copy.6 = f32[3,8,16,128]{3,2,1,0:T(8,128)} copy(f32[3,8,16,128]{3,2,1,0:T(8,128)S(1)} %shard_map.46) | data formatting | bytes 393216

commit v6 on v5

--- a/solution.py
+++ b/solution.py
@@ -200,18 +200,6 @@
     ]
     near_up, near_down = up, down
     up, down = [], []
-    y_cells = [
-        send(flags.at[:, yfirst], FL.at[xown, yhigh], Y, 2, *SOUTH),
-        send(visc.at[:, ylast], VI.at[xown, ylow], Y, 3, *NORTH),
-        send(visc.at[:, yfirst], VI.at[xown, yhigh], Y, 4, *SOUTH),
-    ]
-    y_started = [
-        send(S.at[w, xown, elast], S.at[w, xown, ylow], Y, 5, *NORTH),
-        send(S.at[u, upper, elast], S.at[u, upper, ylow], Y, 6, *NORTH),
-        send(S.at[w, xown, efirst], S.at[w, xown, yhigh], Y, 7, *SOUTH),
-        send(S.at[u, upper, efirst], S.at[u, upper, yhigh], Y, 8, *SOUTH),
-    ]
-
     y_press()
     y_flags()
     for a, b in blocks(X0, X1, 2):
@@ -224,15 +212,26 @@
         send(S.at[v, low3, rows], S.at[v, xhigh, rows], X, 13, *DOWN, later=down),
     ]
     start(up, down, True)
-    y_started += [
-        send(S.at[v, xown, elast], S.at[v, xown, ylow], Y, 9, *NORTH),
-        send(S.at[v, xown, efirst], S.at[v, xown, yhigh], Y, 10, *SOUTH),
-    ]
     for wait, (_, source, target, n) in zip(far_cells, passing[0] + passing[1]):
         wait()
         to, there = ((gx + 2, gy), pass_up) if n % 2 == 0 else ((gx - 2, gy), pass_down)
         send(source, target, X, n, to, there, None, out=19 + n)
     start(near_up + up, near_down + down, False)
+    y_cells = [
+        send(flags.at[:, yfirst], FL.at[xown, yhigh], Y, 2, *SOUTH),
+        send(visc.at[:, ylast], VI.at[xown, ylow], Y, 3, *NORTH),
+        send(visc.at[:, yfirst], VI.at[xown, yhigh], Y, 4, *SOUTH),
+    ]
+    y_started = [
+        send(S.at[w, xown, elast], S.at[w, xown, ylow], Y, 5, *NORTH),
+        send(S.at[u, upper, elast], S.at[u, upper, ylow], Y, 6, *NORTH),
+        send(S.at[w, xown, efirst], S.at[w, xown, yhigh], Y, 7, *SOUTH),
+        send(S.at[u, upper, efirst], S.at[u, upper, yhigh], Y, 8, *SOUTH),
+    ]
+    y_started += [
+        send(S.at[v, xown, elast], S.at[v, xown, ylow], Y, 9, *NORTH),
+        send(S.at[v, xown, efirst], S.at[v, xown, yhigh], Y, 10, *SOUTH),
+    ]
 
     local[3].wait()
     n = 11
@@ -321,7 +320,7 @@
 
     zero = jnp.zeros((1, EY, NZ), F32)
     b0 = h00 = h01 = h11 = h12 = h22 = zero
-    for a, b in blocks(1, EX - 1, 4):
+    for a, b in blocks(1, EX - 1, 7):
         grad, _ = gradient(S, a, b)
         total = 0.0
         for c in range(3):
@@ -329,7 +328,7 @@
             V0[c, a:b] = z
             total = total - z * grad[c]
         b0 = b0 + partial(total, a, b, inside)
-    for a, b in blocks(2, EX - 2, 4):
+    for a, b in blocks(2, EX - 2, 6):
         grad, field = gradient(V0, a, b)
         same = cross = 0.0
         for c in range(3):
@@ -338,7 +337,7 @@
             V1[c, a:b] = z
             same, cross = same + field[c] * g, cross + z * g
         h00, h01 = h00 + partial(same, a, b, inside), h01 + partial(cross, a, b, inside)
-    for a, b in blocks(3, EX - 3, 4):
+    for a, b in blocks(3, EX - 3, 5):
         grad, field = gradient(V1, a, b)
         same = cross = 0.0
         for c in range(3):

time: 50.3 us -> 50.2 us (level)
  no operation moved by 1% of the time
where the time goes in v6:
time: 50.2 us; the launch traced here: 50 us
  Pallas kernels  49.3 us (98%)
  local copies, waits for them, and re-layouts  0.68 us (1%)
    pallas_call x1, Pallas kernels, local(): pl.pallas_call(body, out_shape=jax.ShapeDtypeStruct((3, NX, NY, NZ), F32)...  49.3 us

profile of v6, /device:TPU:1, one launch (start us, length us, event | category | flops | bytes accessed | tf_op | source)
XLA Modules:
  0.0 50.0 jit_solution(14958365195597152396)
XLA Ops:
  0.0 49.3 %shard_map.46 = f32[3,8,16,128]{3,2,1,0:T(8,128)S(1)} custom-call(f32[3,8,16,128]{3,2,1,0:T(8,128)} %refs_0_.1, f32[8,16,128]{2,1,0:T(8,128)} %refs_1_.1, f32[8,16,128]{2,1,0:T(8,128)} %refs_2_.1, s32[8,16,128]{2,1,0:T(8,128)} %refs_3_.1), custom_call_target="tpu_custom_call" | custom-call | tf_op jit(solution)/shard_map/pallas_call | solution.py:451
  49.4 0.7 %copy.6 = f32[3,8,16,128]{3,2,1,0:T(8,128)} copy(f32[3,8,16,128]{3,2,1,0:T(8,128)S(1)} %shard_map.46) | data formatting | bytes 393216

commit v7 on v6

--- a/solution.py
+++ b/solution.py
@@ -12,7 +12,7 @@
 EX, EY = NX + LOW + HIGH, 24
 X0, X1 = LOW, LOW + NX
 Y0, Y1 = LOW, LOW + NY
-CARD, RING = 32, 16
+CARD, RING = 16, 32
 
 
 def low_y(a):
@@ -56,20 +56,20 @@
     ylo, yhi = (gx, gy - 1), (gx, gy + 1)
     px, zh, py = gx // 8, lax.rem(gx // 4, 2), lax.rem(gx, 4)
     zl, core = gy // 2, lax.rem(gy, 2)
-    card = (px * 4 + py) * 2 + core
-    ring = zh * 8 + zl
+    card = px * 4 + py
+    ring = (zh * 8 + zl) * 2 + core
 
     def hops(d, n):
         return min(d, n - d)
 
-    steps = [(dx, dy, dc) for dx in range(4) for dy in range(4) for dc in range(2)]
+    steps = [(dx, dy, dc) for dx in range(4) for dy in range(4) for dc in range(1)]
     steps.sort(key=lambda d: -(hops(d[0], 4) + hops(d[1], 4) + 0.3 * d[2]))
     pxs, pys, cores = [lax.rem(px + d, 4) * 8 for d in range(4)], [lax.rem(py + d, 4) for d in range(4)], (core, 1 - core)
     card_peers = [(pxs[dx] + zh * 4 + pys[dy], zl * 2 + cores[dc]) for dx, dy, dc in steps[:-1]]
     ring_peers = []
-    for d in sorted(range(1, RING), key=lambda d: -hops(d, RING)):
-        z = lax.rem(ring + d, RING)
-        ring_peers.append((px * 8 + (z // 8) * 4 + py, lax.rem(z, 8) * 2 + core))
+    for d in sorted(range(16), key=lambda d: -hops(d, 16)):
+        z = lax.rem(zh * 8 + zl + d, 16)
+        ring_peers += [(px * 8 + (z // 8) * 4 + py, lax.rem(z, 8) * 2 + c) for c in (cores if d else cores[1:])]
 
     own = (pl.ds(X0, NX), pl.ds(Y0, NY))
     local = [

time: 50.2 us -> 50.1 us (level)
  no operation moved by 1% of the time
where the time goes in v7:
time: 50.1 us; the launch traced here: 49.9 us
  Pallas kernels  49.2 us (98%)
  local copies, waits for them, and re-layouts  0.68 us (1%)
    pallas_call x1, Pallas kernels, local(): pl.pallas_call(body, out_shape=jax.ShapeDtypeStruct((3, NX, NY, NZ), F32)...  49.2 us

profile of v7, /device:TPU:1, one launch (start us, length us, event | category | flops | bytes accessed | tf_op | source)
XLA Modules:
  0.0 49.9 jit_solution(388908903324812960)
XLA Ops:
  0.0 49.2 %shard_map.46 = f32[3,8,16,128]{3,2,1,0:T(8,128)S(1)} custom-call(f32[3,8,16,128]{3,2,1,0:T(8,128)} %refs_0_.1, f32[8,16,128]{2,1,0:T(8,128)} %refs_1_.1, f32[8,16,128]{2,1,0:T(8,128)} %refs_2_.1, s32[8,16,128]{2,1,0:T(8,128)} %refs_3_.1), custom_call_target="tpu_custom_call" | custom-call | tf_op jit(solution)/shard_map/pallas_call | solution.py:451
  49.3 0.7 %copy.6 = f32[3,8,16,128]{3,2,1,0:T(8,128)} copy(f32[3,8,16,128]{3,2,1,0:T(8,128)S(1)} %shard_map.46) | data formatting | bytes 393216
